TPU v7x, 512 devices: a whole 4x4x16 slice. The times are simulated.
512 devices in a mesh: tm: 16 (over y, x_hi, core), tile: 32 (over x_lo, z).
Axes of the slice: x: 4 (x_hi: 2, x_lo: 2; x = x_hi * 2 + x_lo), y: 4, z: 16, core: 2. Of those that a mesh axis runs over, the one named last changes fastest.
Arguments:
- latent: bfloat16 [16, 512, 256], P('tm', 'tile'), may hold values from -48 to 48
- conv_weight: bfloat16 [512, 4, 4, 4, 512], P('tile'), may hold values from -0.09375 to 0.09375
- conv_bias: float32 [512], P('tile'), may hold values from -3 to 3
- query_weight: bfloat16 [16, 128, 128], replicated, may hold values from -3 to 3
- key_weight: bfloat16 [16, 128, 128], replicated, may hold values from -3 to 3
Outputs:
- attended: bfloat16 [512, 256, 128], P(('tm', 'tile'))
All inputs are finite; a program needn't handle non-finite values.
Results may differ from a plain program's by a relative error of at most 0.0085.
Values may be sent and summed in bfloat16 or wider, within the bound.
No kernel may reach another device: no remote copies, remote signals or barrier semaphores. Data moves between devices by JAX's collectives and lax.ppermute only.
A program may use at most 64 MiB of HBM per device.

v0:
```python
import jax
import jax.numpy as jnp
from jax import lax
from jax.sharding import PartitionSpec as P

HEADS = 16
SIDE = 16


def passed_along(block, axis, distance):
    devices = range(lax.axis_size(axis))
    route = [(i - distance, i) for i in devices if i - distance in devices]
    return lax.ppermute(block, axis, route)


def spread_taps(products, side_cells):
    combined = 0.0
    for shift_y in (0, 1):
        for shift_x in (0, 1):
            piece_term = products[:, :, shift_y, :, shift_x, :, :, :]
            piece_term = jnp.transpose(piece_term, (0, 1, 4, 2, 5, 3))
            piece_term = jnp.pad(
                piece_term,
                ((0, 0), (0, 0), (shift_y, 1 - shift_y), (0, 0), (shift_x, 1 - shift_x), (0, 0)),
            )
            combined = combined + piece_term
    channels = products.shape[0]
    tap_count = products.shape[1]
    cropped = combined.reshape(channels, tap_count, 2 * side_cells + 2, 2 * side_cells + 2)[
        :, :, 1:-1, 1:-1
    ]
    return cropped.reshape(channels, tap_count, 4 * side_cells * side_cells)


def conv_taps(latent_plane, weight_rows, side_cells):
    channels = weight_rows.shape[0]
    tap_count = weight_rows.shape[1]
    products = jnp.dot(
        weight_rows.reshape(-1, weight_rows.shape[-1]),
        latent_plane,
        preferred_element_type=jnp.float32,
    )
    products = products.reshape(channels, tap_count, 2, 2, 2, 2, side_cells, side_cells)
    return spread_taps(products, side_cells)


def attend_pair(items):
    token_rows, query_tokens, query_rows, key_rows = items
    queries = jnp.dot(query_tokens, query_rows, preferred_element_type=jnp.float32).astype(
        jnp.bfloat16
    )
    projected = jnp.dot(token_rows, key_rows, preferred_element_type=jnp.float32).astype(
        jnp.bfloat16
    )
    scale = token_rows.shape[1] ** (-0.5)
    row_count = query_tokens.shape[0]

    def one_block(block_items):
        query_block, token_block = block_items
        scores = jnp.dot(query_block, projected.T, preferred_element_type=jnp.float32) * scale
        weights = jax.nn.softmax(scores, axis=-1).astype(jnp.bfloat16)
        mixed = jnp.dot(weights, token_rows, preferred_element_type=jnp.float32)
        return (token_block.astype(jnp.float32) + mixed).astype(jnp.bfloat16)

    block_count = row_count // row_count
    result = lax.map(
        one_block,
        (
            queries.reshape(block_count, row_count, -1),
            query_tokens.reshape(block_count, row_count, -1),
        ),
    )
    return result.reshape(row_count, -1)


def local(latent, conv_weight, conv_bias, query_weight, key_weight):
    prev_frame = passed_along(latent, "tm", 1)
    next_frame = passed_along(latent, "tm", -1)
    gathered = lax.all_gather(
        jnp.concatenate([prev_frame, latent, next_frame], 0), "tile", axis=1, tiled=True
    )
    own_taps = conv_taps(gathered[1], conv_weight[:, 1:3], SIDE)
    edge_taps = jnp.concatenate(
        [
            conv_taps(gathered[0], conv_weight[:, 3:4], SIDE),
            conv_taps(gathered[2], conv_weight[:, 0:1], SIDE),
        ],
        1,
    )
    summed = own_taps + edge_taps
    frames = (summed + conv_bias[:, None, None]).astype(jnp.bfloat16)
    local_channels = frames.shape[0]
    pixels = frames.shape[2]
    per_head = local_channels // HEADS
    tile_count = lax.axis_size("tile")
    qsplit = max(1, tile_count // (2 * HEADS))
    arranged = frames.reshape(per_head, HEADS, 2, pixels)
    arranged = jnp.transpose(arranged, (2, 1, 0, 3)).reshape(2 * HEADS, per_head, pixels)
    received = lax.all_to_all(arranged, "tile", split_axis=0, concat_axis=1, tiled=True)
    pair_count = received.shape[0]
    head_chan = received.shape[1]
    tokens = received.reshape(pair_count, head_chan, SIDE, 2, SIDE, 2)
    tokens = jnp.transpose(tokens, (0, 2, 4, 3, 5, 1)).reshape(
        pair_count, SIDE * SIDE, 4 * head_chan
    )
    tile_index = lax.axis_index("tile")
    head_start = tile_index * pair_count // qsplit % HEADS
    query_rows = lax.dynamic_slice_in_dim(query_weight, head_start, pair_count, 0)
    key_rows = lax.dynamic_slice_in_dim(key_weight, head_start, pair_count, 0)
    return lax.map(attend_pair, (tokens, tokens, query_rows, key_rows))


def solution(mesh):
    in_specs = (P("tm", "tile", None), P("tile", None, None, None, None), P("tile"), P(), P())
    out_specs = P(("tm", "tile"), None, None)
    return jax.shard_map(local, mesh=mesh, in_specs=in_specs, out_specs=out_specs, check_vma=False)
```

profile of v0, /device:TPU:24, one launch (start us, length us, event | category | flops | bytes accessed | tf_op | source)
XLA Modules:
  0.0 126.5 jit_solution(12531573350634435068)
XLA Ops:
  0.0 2.0 %collective-permute-start = (bf16[1,16,256]{2,1,0:T(8,128)(2,1)}, bf16[1,16,256]{2,1,0:T(8,128)(2,1)S(1)}, u32[]{:S(2)}, u32[]{:S(2)}) collective-permute-start(bf16[1,16,256]{2,1,0:T(8,128)(2,1)} %param.5), channel_id=1, source_target_pairs={{0,32},{32,64},{64,96},{96,128},{128,160},{160,192},{192,224},{224... | collective-permute-start | bytes 24584 | tf_op jit(solution)/shard_map/ppermute | solution.py:13
  2.1 6.0 %collective-permute-start.1 = (bf16[1,16,256]{2,1,0:T(8,128)(2,1)}, bf16[1,16,256]{2,1,0:T(8,128)(2,1)S(1)}, u32[]{:S(2)}, u32[]{:S(2)}) collective-permute-start(bf16[1,16,256]{2,1,0:T(8,128)(2,1)} %param.5), channel_id=1, source_target_pairs={{32,0},{64,32},{96,64},{128,96},{160,128},{192,160},{224,192},{256... | collective-permute-start | bytes 24584 | tf_op jit(solution)/shard_map/ppermute | solution.py:13
  8.1 1.3 fusion.16
  9.5 0.8 reshape.106
  10.2 0.9 reshape.99
  11.2 73.2 %all_gather.3 = bf16[3,512,256]{2,1,0:T(8,128)(2,1)S(1)} all-gather(bf16[3,16,256]{2,1,0:T(8,128)(2,1)S(1)} %pad_maximum_fusion), channel_id=1, replica_groups=mesh['tm'=16,'tile'=32] {'tile'}, dimensions={1}, use_global_device_ids=true | all-gather | bytes 811008 | tf_op jit(solution)/shard_map/all_gather | solution.py:79
  84.3 0.3 convolution_bitcast_fusion.2
  84.6 0.8 copy.40
  85.4 1.7 %reshape.104 = f32[16,1,2,2,2,2,16,16]{7,6,5,4,3,2,0,1:T(8,128)S(1)} reshape(f32[256,256]{1,0:T(8,128)} %copy.40) | data formatting | bytes 524288 | tf_op jit(solution)/shard_map/reshape | solution.py:43
  87.3 0.4 pad_add_fusion.2
  87.7 0.7 copy.44
  88.6 0.7 copy-done.2
  89.3 0.3 convolution_bitcast_fusion.1
  89.6 0.8 copy.45
  90.5 1.7 %reshape.107 = f32[16,1,2,2,2,2,16,16]{7,6,5,4,3,2,0,1:T(8,128)S(1)} reshape(f32[256,256]{1,0:T(8,128)} %copy.45) | data formatting | bytes 524288 | tf_op jit(solution)/shard_map/reshape | solution.py:43
  92.3 0.4 pad_add_fusion.1
  92.7 0.7 copy.49
  93.8 0.3 convolution_bitcast_fusion
  94.3 2.6 %reshape.100 = f32[16,2,2,2,2,2,16,16]{7,6,5,4,3,2,1,0:T(8,128)} reshape(f32[512,256]{1,0:T(8,128)S(1)} %copy.35) | data formatting | bytes 1048576 | tf_op jit(solution)/shard_map/reshape | solution.py:43
  97.0 2.6 %slice_bitcast_fusion.3 = (f32[16,2,16,2,16,2]{4,2,5,3,1,0:T(8,128)S(1)}, f32[16,2,16,2,16,2]{4,2,5,3,1,0:T(8,128)S(1)}, f32[16,2,16,2,16,2]{4,2,5,3,1,0:T(8,128)S(1)}, f32[16,2,16,2,16,2]{4,2,5,3,1,0:T(8,128)S(1)}) fusion(f32[16,2,2,2,2,2,16,16]{7,6,5,4,3,2,1,0:T(8,128)} %reshape.100), kind=kLoop, calls=%fused_computation.13 | loop fusion | bytes 1048576 | tf_op jit(solution)/shard_map/transpose | solution.py:21
  99.6 0.8 pad_add_fusion
  100.4 2.4 %copy.39 = f32[16,2,17,2,17,2]{0,1,5,4,3,2:T(2,128)S(1)} copy(f32[16,2,17,2,17,2]{4,2,5,3,1,0:T(8,128)S(1)} %pad_add_fusion) | data formatting | bytes 295936 | tf_op jit(solution)/shard_map/add | solution.py:26
  103.0 0.4 copy.52
  103.6 0.5 broadcast.49
  104.1 0.7 reduce
  104.7 0.7 reshape.111
  105.4 3.9 %all-to-all-start = ((bf16[32,2,512]{2,1,0:T(2,128)(2,1)}), bf16[32,2,512]{2,1,0:T(2,128)(2,1)S(1)}, u32[]{:S(2)}, u32[]{:S(2)}) async-start(bf16[32,2,512]{2,1,0:T(2,128)(2,1)} %reshape.111), calls=%async_computation | async-start | bytes 131072 | tf_op jit(solution)/shard_map/all_to_all | solution.py:99
  109.3 14.3 %all-to-all-done = bf16[32,2,512]{2,1,0:T(2,128)(2,1)S(1)} async-done(((bf16[32,2,512]{2,1,0:T(2,128)(2,1)}), bf16[32,2,512]{2,1,0:T(2,128)(2,1)S(1)}, u32[]{:S(2)}, u32[]{:S(2)}) %all-to-all-start) | async-done | bytes 65568 | tf_op jit(solution)/shard_map/all_to_all | solution.py:99
  123.9 0.2 copy.55
  124.2 0.9 convolution_convert_fusion
  125.2 0.4 fusion.17
  125.6 0.9 fusion.1
  (28 shorter events, 2.0 us)
Async XLA Ops:
  0.0 125.2 %copy-start = (bf16[16,128,128]{2,1,0:T(8,128)(2,1)S(1)}, bf16[16,128,128]{2,1,0:T(8,128)(2,1)}, u32[]{:S(2)}) copy-start(bf16[16,128,128]{2,1,0:T(8,128)(2,1)} %param.8) | copy-start | bytes 1572868
  0.0 10.2 %slice-start = ((bf16[16,4,4,4,512]{4,3,2,1,0:T(4,128)(2,1)}), bf16[16,2,4,4,512]{4,3,2,1,0:T(4,128)(2,1)S(1)}, s32[]{:S(2)}) async-start(bf16[16,4,4,4,512]{4,3,2,1,0:T(4,128)(2,1)} %param.6), calls=%async_computation.1 | async-start | bytes 1048576 | tf_op jit(solution)/shard_map/slice | solution.py:82
  0.0 11.1 %collective-permute-start = (bf16[1,16,256]{2,1,0:T(8,128)(2,1)}, bf16[1,16,256]{2,1,0:T(8,128)(2,1)S(1)}, u32[]{:S(2)}, u32[]{:S(2)}) collective-permute-start(bf16[1,16,256]{2,1,0:T(8,128)(2,1)} %param.5), channel_id=1, source_target_pairs={{0,32},{32,64},{64,96},{96,128},{128,160},{160,192},{192,224},{224... | collective-permute-start | bytes 24584 | tf_op jit(solution)/shard_map/ppermute | solution.py:13
  2.1 9.1 %collective-permute-start.1 = (bf16[1,16,256]{2,1,0:T(8,128)(2,1)}, bf16[1,16,256]{2,1,0:T(8,128)(2,1)S(1)}, u32[]{:S(2)}, u32[]{:S(2)}) collective-permute-start(bf16[1,16,256]{2,1,0:T(8,128)(2,1)} %param.5), channel_id=1, source_target_pairs={{32,0},{64,32},{96,64},{128,96},{160,128},{192,160},{224,192},{256... | collective-permute-start | bytes 24584 | tf_op jit(solution)/shard_map/ppermute | solution.py:13
  9.4 1.8 %copy-start.3 = (bf16[1,16,256]{2,1,0:T(8,128)(2,1)S(1)}, bf16[1,16,256]{2,1,0:T(8,128)(2,1)}, u32[]{:S(2)}) copy-start(bf16[1,16,256]{2,1,0:T(8,128)(2,1)} %param.5) | copy-start | bytes 24580
  88.4 1.0 copy-start.2
  92.7 1.0 copy-start.1
  102.8 0.7 copy-start.4
  105.4 18.2 %all-to-all-start = ((bf16[32,2,512]{2,1,0:T(2,128)(2,1)}), bf16[32,2,512]{2,1,0:T(2,128)(2,1)S(1)}, u32[]{:S(2)}, u32[]{:S(2)}) async-start(bf16[32,2,512]{2,1,0:T(2,128)(2,1)} %reshape.111), calls=%async_computation | async-start | bytes 131072 | tf_op jit(solution)/shard_map/all_to_all | solution.py:99
where the time goes:
time: 127 us; the launch traced here: 126 us
  blocking collectives  73.2 us (58%)
  local copies, waits for them, and re-layouts  21.4 us (17%)
  waiting for transfers between devices  14.3 us (11%)
  starting transfers between devices  11.9 us (9%)
  matrix products  3.04 us (2%)
  other arithmetic  2.39 us (2%)
    all_gather x1, blocking collectives, local(): lax.all_gather(jnp.concatenate([prev_frame, latent, next_frame], 0), 'til...  73.2 us
    all_to_all x1, waiting for transfers between devices, local(): lax.all_to_all(arranged, 'tile', split_axis=0, concat_axis=1, tiled=True)  14.3 us
    ppermute x2, starting transfers between devices, passed_along(): return lax.ppermute(block, axis, route)  8.09 us
    reshape x3, local copies, waits for them, and re-layouts, conv_taps(): products.reshape(channels, tap_count, 2, 2, 2, 2, side_cells, side_cells)  5.95 us
    all_to_all x1, starting transfers between devices, local(): lax.all_to_all(arranged, 'tile', split_axis=0, concat_axis=1, tiled=True)  3.86 us
    add x3, local copies, waits for them, and re-layouts, spread_taps(): combined = combined + piece_term  3.84 us
    transpose x3, local copies, waits for them, and re-layouts, spread_taps(): piece_term = jnp.transpose(piece_term, (0, 1, 4, 2, 5, 3))  3.01 us
  transfers between devices with their start and end apart: 3, of which 1 were waited for; matrix products, arithmetic and copies ran while one was open for 2% of the time, Pallas kernels for 0%

commit v1 on v0

v1 whole, which is shorter than its diff:
```python
import jax
import jax.numpy as jnp
from jax import lax
from jax.experimental import pallas as pl
from jax.experimental.pallas import tpu as pltpu
from jax.sharding import Mesh, PartitionSpec as P

HEADS = 16
SIDE = 16
CELLS = SIDE * SIDE
TM = ("pair", "core")
VMEM_LIMIT = 32 * 1024 * 1024


def spread(tap_slabs, channels):
    lane = lax.broadcasted_iota(jnp.int32, (channels, CELLS), 1)
    row, col = lane // SIDE, lane % SIDE
    for pa in (0, 1):
        for pb in (0, 1):
            total = None
            for ky, dy in ((1, 0), (3, -1)) if pa == 0 else ((2, 0), (0, 1)):
                for kx, dx in ((1, 0), (3, -1)) if pb == 0 else ((2, 0), (0, 1)):
                    slab = tap_slabs(ky, kx)
                    step = dy * SIDE + dx
                    if step:
                        slab = pltpu.roll(slab, (-step) % CELLS, 1)
                        inside = (row + dy >= 0) & (row + dy < SIDE) & (col + dx >= 0) & (col + dx < SIDE)
                        slab = jnp.where(inside, slab, 0.0)
                    total = slab if total is None else total + slab
            yield pa, pb, total


def conv_kernel(core_ref, weight_ref, latent_ref, bias_ref, own_ref, near_ref, far_ref, later_ref, earlier_ref):
    channels = bias_ref.shape[0]
    rows = 16 * channels
    latent = latent_ref[...]
    for kt in (3, 0, 1, 2):
        products = jnp.dot(
            weight_ref[kt * rows : (kt + 1) * rows, :], latent, preferred_element_type=jnp.float32
        )

        def tap(ky, kx):
            start = (ky * 4 + kx) * channels
            return products[start : start + channels, :]

        for pa, pb, total in spread(tap, channels):
            if kt in (1, 2):
                total = total + bias_ref[...]
            for half in (0, 1):
                piece = total[:, half * 128 : (half + 1) * 128]
                place = (pa * 2 + pb) * 2 + half
                if kt == 3:
                    later_ref[:, place, :] = piece
                elif kt == 0:
                    earlier_ref[:, place, :] = piece
                else:
                    own_ref[kt - 1, :, place, :] = piece
    first = core_ref[0] == 0
    later, earlier = later_ref[...], earlier_ref[...]
    near_ref[...] = jnp.where(first, later, earlier).astype(jnp.bfloat16)
    far_ref[...] = jnp.where(first, earlier, later).astype(jnp.bfloat16)


def attend_kernel(piece_ref, query_ref, key_ref, out_ref, wide_ref, turned_ref):
    wide_ref[...] = piece_ref[...].astype(jnp.float32)
    channels = wide_ref.shape[0]
    for place in range(8):
        parity, half = place // 2, place % 2
        turned_ref[parity * channels : (parity + 1) * channels, half * 128 : (half + 1) * 128] = wide_ref[:, place, :]
    wide = turned_ref[...].T
    tokens = wide.astype(jnp.bfloat16)
    queries = jnp.dot(tokens, query_ref[...], preferred_element_type=jnp.float32).astype(jnp.bfloat16)
    keys = jnp.dot(tokens, key_ref[...], preferred_element_type=jnp.float32).astype(jnp.bfloat16)
    scores = lax.dot_general(queries, keys, (((1,), (1,)), ((), ())), preferred_element_type=jnp.float32)
    scores = scores * (tokens.shape[1] ** -0.5)
    raised = jnp.exp(scores - jnp.max(scores, axis=1, keepdims=True))
    weights = (raised / jnp.sum(raised, axis=1, keepdims=True)).astype(jnp.bfloat16)
    mixed = jnp.dot(weights, tokens, preferred_element_type=jnp.float32)
    out_ref[...] = (wide + mixed).astype(jnp.bfloat16)


def local(latent, conv_weight, conv_bias, query_weight, key_weight):
    tiles = lax.axis_size("tile")
    channels = conv_weight.shape[0]
    core = lax.axis_index("core").astype(jnp.int32)
    copies = jnp.broadcast_to(latent, (tiles,) + latent.shape[1:])
    gathered = lax.all_to_all(copies, "tile", split_axis=0, concat_axis=0, tiled=True)
    gathered = gathered.reshape(-1, CELLS)
    rows = jnp.transpose(conv_weight, (1, 2, 3, 0, 4)).reshape(-1, conv_weight.shape[-1])
    head = lax.axis_index("tile") % HEADS
    query_rows = lax.dynamic_index_in_dim(query_weight, head, 0, keepdims=False)
    key_rows = lax.dynamic_index_in_dim(key_weight, head, 0, keepdims=False)

    edge = jax.ShapeDtypeStruct((channels, 8, 128), jnp.bfloat16)
    own, near, far = pl.pallas_call(
        conv_kernel,
        out_shape=(jax.ShapeDtypeStruct((2, channels, 8, 128), jnp.float32), edge, edge),
        in_specs=[pl.BlockSpec(memory_space=pltpu.SMEM)] + [pl.BlockSpec(memory_space=pltpu.VMEM)] * 3,
        out_specs=[pl.BlockSpec(memory_space=pltpu.VMEM)] * 3,
        scratch_shapes=[pltpu.VMEM((channels, 8, 128), jnp.float32)] * 2,
        compiler_params=pltpu.CompilerParams(vmem_limit_bytes=VMEM_LIMIT),
        name="conv",
    )(core.reshape(1), rows, gathered, conv_bias.reshape(channels, 1))

    groups = lax.axis_size("pair") * lax.axis_size("core")
    route = [(t, t + 1) for t in range(1, groups - 1, 2)] + [(t + 1, t) for t in range(1, groups - 1, 2)]
    from_far = lax.ppermute(far, TM, route)
    both = lax.all_gather(near, "core", axis=0)
    from_near = jnp.where(core == 0, both[1], both[0])
    to_first = jnp.where(core == 0, from_far, from_near).astype(jnp.float32)
    to_second = jnp.where(core == 0, from_near, from_far).astype(jnp.float32)
    frames = (own + jnp.stack([to_first, to_second])).astype(jnp.bfloat16)
    received = lax.all_to_all(
        frames.reshape(2 * channels, 8, 128), "tile", split_axis=0, concat_axis=0, tiled=True
    )
    vmem = pl.BlockSpec(memory_space=pltpu.VMEM)
    attended = pl.pallas_call(
        attend_kernel,
        out_shape=jax.ShapeDtypeStruct((CELLS, 4 * tiles), jnp.bfloat16),
        in_specs=[vmem] * 3,
        out_specs=vmem,
        scratch_shapes=[pltpu.VMEM((tiles, 8, 128), jnp.float32), pltpu.VMEM((4 * tiles, CELLS), jnp.float32)],
        compiler_params=pltpu.CompilerParams(vmem_limit_bytes=VMEM_LIMIT),
        name="attend",
    )(received, query_rows, key_rows)
    return attended[None]


def solution(mesh):
    split = Mesh(mesh.devices.reshape(-1, 2, mesh.devices.shape[1]), ("pair", "core", "tile"))
    in_specs = (P(TM, "tile", None), P("tile", None, None, None, None), P("tile"), P(), P())
    out_specs = P(TM + ("tile",), None, None)
    return jax.shard_map(local, mesh=split, in_specs=in_specs, out_specs=out_specs, check_vma=False)
```

time: 127 us -> 69 us (0.54)
  blocking collectives: 73.2 us -> 4.34 us
  waiting for transfers between devices: 14.3 us -> 34.5 us
  local copies, waits for them, and re-layouts: 21.4 us -> 4.73 us
  starting transfers between devices: 11.9 us -> 22.2 us
  matrix products: 3.04 us -> 0 us
  Pallas kernels: 0 us -> 2.08 us
  other arithmetic: 2.39 us -> 0.66 us
    all_gather x1, blocking collectives: 73.2 us -> 4.34 us  [local(): both = lax.all_gather(near, 'core', axis=0)]
    all_to_all x1 -> x2, waiting for transfers between devices: 14.3 us -> 33.1 us  [the longest x1 19.7 us: local(): lax.all_to_all(copies, 'tile', split_axis=0, concat_axis=0, tiled=True)]
    all_to_all x1 -> x2, starting transfers between devices: 3.86 us -> 20.3 us  [the longest x1 16.4 us: local(): lax.all_to_all(copies, 'tile', split_axis=0, concat_axis=0, tiled=True)]
    reshape x8 -> x1, local copies, waits for them, and re-layouts: 8.63 us -> 0.08 us  [local(): conv_bias.reshape(channels, 1)]
    ppermute x2 -> x1, starting transfers between devices: 8.09 us -> 1.92 us  [local(): from_far = lax.ppermute(far, TM, route)]
    add x3 -> x0, local copies, waits for them, and re-layouts: 3.84 us -> none  [spread_taps(): combined = combined + piece_term]
    dot_general x6 -> x0, matrix products: 3.04 us -> none  [the longest x1 0.91 us: attend_pair(): jnp.dot(token_rows, key_rows, preferred_element_type=jnp.float32)]
    pallas_call x0 -> x2, Pallas kernels: none -> 2.08 us  [the longest x1 1.45 us: local(): pl.pallas_call(attend_kernel, out_shape=jax.ShapeDtypeStruct((CELLS, 4 *...]
  transfers between devices with their start and end apart: 3 -> 3, of which waited for: 1 -> 3; matrix products, arithmetic and copies ran while one was open for 2% -> 4% of each run, Pallas kernels for 0% -> 0%
where the time goes in v1:
time: 69 us; the launch traced here: 68.6 us
  waiting for transfers between devices  34.5 us (50%)
  starting transfers between devices  22.2 us (32%)
  local copies, waits for them, and re-layouts  4.73 us (7%)
  blocking collectives  4.34 us (6%)
  Pallas kernels  2.08 us (3%)
    all_to_all x1, waiting for transfers between devices, local(): lax.all_to_all(copies, 'tile', split_axis=0, concat_axis=0, tiled=True)  19.7 us
    all_to_all x1, starting transfers between devices, local(): lax.all_to_all(copies, 'tile', split_axis=0, concat_axis=0, tiled=True)  16.4 us
    all_to_all x1, waiting for transfers between devices, local(): lax.all_to_all(frames.reshape(2 * channels, 8, 128), 'tile', split_axis=0...  13.5 us
    all_gather x1, blocking collectives, local(): both = lax.all_gather(near, 'core', axis=0)  4.34 us
    all_to_all x1, starting transfers between devices, local(): lax.all_to_all(frames.reshape(2 * channels, 8, 128), 'tile', split_axis=0...  3.86 us
    ppermute x1, starting transfers between devices, local(): from_far = lax.ppermute(far, TM, route)  1.92 us
    transpose x1, local copies, waits for them, and re-layouts, local(): jnp.transpose(conv_weight, (1, 2, 3, 0, 4))  1.81 us
    pallas_call x1, Pallas kernels, local(): pl.pallas_call(attend_kernel, out_shape=jax.ShapeDtypeStruct((CELLS, 4 *...  1.45 us
  transfers between devices with their start and end apart: 3, of which 3 were waited for; matrix products, arithmetic and copies ran while one was open for 4% of the time, Pallas kernels for 0%

profile of v1, /device:TPU:24, one launch (start us, length us, event | category | flops | bytes accessed | tf_op | source)
XLA Modules:
  0.0 68.6 jit_solution(18045686971261829733)
XLA Ops:
  0.0 1.4 %broadcast_in_dim.11 = bf16[32,16,256]{2,1,0:T(8,128)(2,1)} broadcast(bf16[16,256]{1,0:T(8,128)(2,1)} %bitcast.19), dimensions={1,2} | broadcast | bytes 270336 | tf_op jit(solution)/shard_map/broadcast_in_dim | solution.py:86
  1.4 16.4 %all-to-all-start = ((bf16[32,16,256]{2,1,0:T(8,128)(2,1)}), bf16[32,16,256]{2,1,0:T(8,128)(2,1)S(1)}, u32[]{:S(2)}, u32[]{:S(2)}) async-start(bf16[32,16,256]{2,1,0:T(8,128)(2,1)} %broadcast_in_dim.11), calls=%async_computation | async-start | bytes 524288 | tf_op jit(solution)/shard_map/all_to_all | solution.py:87
  17.8 0.0 copy-start
  17.8 0.6 copy-done
  18.5 0.1 copy.9.bias_ref
  18.6 1.8 %copy.8 = bf16[4,4,4,16,512]{4,3,2,1,0:T(8,128)(2,1)S(1)} copy(bf16[4,4,4,16,512]{4,2,1,0,3:T(4,128)(2,1)} %bitcast.18) | data formatting | bytes 2097152 | tf_op jit(solution)/shard_map/transpose | solution.py:89
  20.4 19.7 %all-to-all-done = bf16[32,16,256]{2,1,0:T(8,128)(2,1)S(1)} async-done(((bf16[32,16,256]{2,1,0:T(8,128)(2,1)}), bf16[32,16,256]{2,1,0:T(8,128)(2,1)S(1)}, u32[]{:S(2)}, u32[]{:S(2)}) %all-to-all-start) | async-done | bytes 262176 | tf_op jit(solution)/shard_map/all_to_all | solution.py:87
  40.1 0.6 conv.1
  40.7 1.9 %collective-permute-start = (bf16[16,8,128]{2,1,0:T(8,128)(2,1)S(1)}, bf16[16,8,128]{2,1,0:T(8,128)(2,1)S(1)}, u32[]{:S(2)}, u32[]{:S(2)}) collective-permute-start(bf16[16,8,128]{2,1,0:T(8,128)(2,1)S(1)} %get-tuple-element.9), channel_id=1, source_target_pairs={{32,64},{96,128},{160,192},{224,256},{288,320},{352,384},{416,448}... | collective-permute-start | bytes 98312 | tf_op jit(solution)/shard_map/ppermute | solution.py:107
  42.6 4.3 %all-gather = bf16[32,8,128]{2,1,0:T(8,128)(2,1)S(1)} all-gather(bf16[16,8,128]{2,1,0:T(8,128)(2,1)S(1)} %get-tuple-element.10), channel_id=2, replica_groups=mesh['pair'=8,'core'=2,'tile'=32] {'core'}, dimensions={0}, use_global_device_ids=true | all-gather | bytes 98304 | tf_op jit(solution)/shard_map/all_gather | solution.py:108
  47.0 1.4 %collective-permute-done = bf16[16,8,128]{2,1,0:T(8,128)(2,1)S(1)} collective-permute-done((bf16[16,8,128]{2,1,0:T(8,128)(2,1)S(1)}, bf16[16,8,128]{2,1,0:T(8,128)(2,1)S(1)}, u32[]{:S(2)}, u32[]{:S(2)}) %collective-permute-start) | collective-permute-done | bytes 32800 | tf_op jit(solution)/shard_map/ppermute | solution.py:107
  48.3 0.6 add_convert_fusion
  49.0 3.9 %all-to-all-start.1 = ((bf16[32,8,128]{2,1,0:T(8,128)(2,1)}), bf16[32,8,128]{2,1,0:T(8,128)(2,1)S(1)}, u32[]{:S(2)}, u32[]{:S(2)}) async-start(bf16[32,8,128]{2,1,0:T(8,128)(2,1)} %bitcast.8), calls=%async_computation.1 | async-start | bytes 131072 | tf_op jit(solution)/shard_map/all_to_all | solution.py:113
  52.9 0.8 %dynamic-slice_bitcast_fusion = (bf16[128,128]{1,0:T(8,128)(2,1)S(1)}, bf16[128,128]{1,0:T(8,128)(2,1)S(1)}) fusion(bf16[16,128,128]{2,1,0:T(8,128)(2,1)} %param.9, s32[]{:T(128)S(6)} %select_n.40, bf16[16,128,128]{2,1,0:T(8,128)(2,1)} %param.8), kind=kLoop, calls=%fused_computation.2 | loop fusion | bytes 131076 | tf_op jit(solution)/shard_map/jit(dynamic_index_in_dim)/squeeze | solution.py:92
  53.7 13.5 %all-to-all-done.1.piece_ref = bf16[32,8,128]{2,1,0:T(8,128)(2,1)S(1)} async-done(((bf16[32,8,128]{2,1,0:T(8,128)(2,1)}), bf16[32,8,128]{2,1,0:T(8,128)(2,1)S(1)}, u32[]{:S(2)}, u32[]{:S(2)}) %all-to-all-start.1) | async-done | bytes 65568 | tf_op jit(solution)/shard_map/all_to_all | solution.py:113
  67.1 1.5 %attend.1 = bf16[256,128]{1,0:T(8,128)(2,1)} custom-call(bf16[32,8,128]{2,1,0:T(8,128)(2,1)S(1)} %all-to-all-done.1.piece_ref, bf16[128,128]{1,0:T(8,128)(2,1)S(1)} %get-tuple-element.14.query_ref, bf16[128,128]{1,0:T(8,128)(2,1)S(1)} %get-tuple-element.13.key_ref), custom_call_target="tpu_custom_call" | custom-call | tf_op jit(solution)/shard_map/attend/pallas_call | solution.py:117
  (1 shorter events, 0.0 us)
Async XLA Ops:
  1.4 38.6 %all-to-all-start = ((bf16[32,16,256]{2,1,0:T(8,128)(2,1)}), bf16[32,16,256]{2,1,0:T(8,128)(2,1)S(1)}, u32[]{:S(2)}, u32[]{:S(2)}) async-start(bf16[32,16,256]{2,1,0:T(8,128)(2,1)} %broadcast_in_dim.11), calls=%async_computation | async-start | bytes 524288 | tf_op jit(solution)/shard_map/all_to_all | solution.py:87
  17.8 0.7 copy-start
  40.7 7.6 %collective-permute-start = (bf16[16,8,128]{2,1,0:T(8,128)(2,1)S(1)}, bf16[16,8,128]{2,1,0:T(8,128)(2,1)S(1)}, u32[]{:S(2)}, u32[]{:S(2)}) collective-permute-start(bf16[16,8,128]{2,1,0:T(8,128)(2,1)S(1)} %get-tuple-element.9), channel_id=1, source_target_pairs={{32,64},{96,128},{160,192},{224,256},{288,320},{352,384},{416,448}... | collective-permute-start | bytes 98312 | tf_op jit(solution)/shard_map/ppermute | solution.py:107
  49.0 18.1 %all-to-all-start.1 = ((bf16[32,8,128]{2,1,0:T(8,128)(2,1)}), bf16[32,8,128]{2,1,0:T(8,128)(2,1)S(1)}, u32[]{:S(2)}, u32[]{:S(2)}) async-start(bf16[32,8,128]{2,1,0:T(8,128)(2,1)} %bitcast.8), calls=%async_computation.1 | async-start | bytes 131072 | tf_op jit(solution)/shard_map/all_to_all | solution.py:113

commit v2 on v1

--- a/solution.py
+++ b/solution.py
@@ -10,6 +10,16 @@
 CELLS = SIDE * SIDE
 TM = ("pair", "core")
 VMEM_LIMIT = 32 * 1024 * 1024
+
+
+def turned(order):
+    half = order // 2
+    tiles = [start + (z + half // 2) % half for start in (0, half) for z in range(half)]
+    return tiles, [tiles.index(tile) for tile in range(order)]
+
+
+def in_turn(blocks, places):
+    return jnp.concatenate([blocks[place] for place in places], 0)
 
 
 def spread(tap_slabs, channels):
@@ -33,7 +43,8 @@
 def conv_kernel(core_ref, weight_ref, latent_ref, bias_ref, own_ref, near_ref, far_ref, later_ref, earlier_ref):
     channels = bias_ref.shape[0]
     rows = 16 * channels
-    latent = latent_ref[...]
+    _, places = turned(latent_ref.shape[0])
+    latent = in_turn(latent_ref, places)
     for kt in (3, 0, 1, 2):
         products = jnp.dot(
             weight_ref[kt * rows : (kt + 1) * rows, :], latent, preferred_element_type=jnp.float32
@@ -54,9 +65,13 @@
                 elif kt == 0:
                     earlier_ref[:, place, :] = piece
                 else:
-                    own_ref[kt - 1, :, place, :] = piece
+                    middle = channels // 2
+                    own_ref[kt - 1, :middle, place, :] = piece[middle:]
+                    own_ref[kt - 1, middle:, place, :] = piece[:middle]
     first = core_ref[0] == 0
-    later, earlier = later_ref[...], earlier_ref[...]
+    middle = channels // 2
+    later = jnp.concatenate([later_ref[middle:], later_ref[:middle]], 0)
+    earlier = jnp.concatenate([earlier_ref[middle:], earlier_ref[:middle]], 0)
     near_ref[...] = jnp.where(first, later, earlier).astype(jnp.bfloat16)
     far_ref[...] = jnp.where(first, earlier, later).astype(jnp.bfloat16)
 
@@ -64,9 +79,13 @@
 def attend_kernel(piece_ref, query_ref, key_ref, out_ref, wide_ref, turned_ref):
     wide_ref[...] = piece_ref[...].astype(jnp.float32)
     channels = wide_ref.shape[0]
+    tiles, _ = turned(channels)
     for place in range(8):
         parity, half = place // 2, place % 2
-        turned_ref[parity * channels : (parity + 1) * channels, half * 128 : (half + 1) * 128] = wide_ref[:, place, :]
+        columns = slice(half * 128, (half + 1) * 128)
+        for run in range(0, channels, 8):
+            start = parity * channels + tiles[run]
+            turned_ref[start : start + 8, columns] = wide_ref[run : run + 8, place, :]
     wide = turned_ref[...].T
     tokens = wide.astype(jnp.bfloat16)
     queries = jnp.dot(tokens, query_ref[...], preferred_element_type=jnp.float32).astype(jnp.bfloat16)
@@ -84,8 +103,8 @@
     channels = conv_weight.shape[0]
     core = lax.axis_index("core").astype(jnp.int32)
     copies = jnp.broadcast_to(latent, (tiles,) + latent.shape[1:])
-    gathered = lax.all_to_all(copies, "tile", split_axis=0, concat_axis=0, tiled=True)
-    gathered = gathered.reshape(-1, CELLS)
+    order, _ = turned(tiles)
+    gathered = lax.all_to_all(copies, "tile", split_axis=0, concat_axis=0, tiled=True, axis_index_groups=[order])
     rows = jnp.transpose(conv_weight, (1, 2, 3, 0, 4)).reshape(-1, conv_weight.shape[-1])
     head = lax.axis_index("tile") % HEADS
     query_rows = lax.dynamic_index_in_dim(query_weight, head, 0, keepdims=False)
@@ -111,7 +130,7 @@
     to_second = jnp.where(core == 0, from_near, from_far).astype(jnp.float32)
     frames = (own + jnp.stack([to_first, to_second])).astype(jnp.bfloat16)
     received = lax.all_to_all(
-        frames.reshape(2 * channels, 8, 128), "tile", split_axis=0, concat_axis=0, tiled=True
+        frames.reshape(2 * channels, 8, 128), "tile", split_axis=0, concat_axis=0, tiled=True, axis_index_groups=[order]
     )
     vmem = pl.BlockSpec(memory_space=pltpu.VMEM)
     attended = pl.pallas_call(

time: 69 us -> 62.7 us (0.909)
  waiting for transfers between devices: 34.5 us -> 15 us
  starting transfers between devices: 22.2 us -> 36.7 us
  blocking collectives: 4.34 us -> 3.07 us
    all_to_all x1, waiting for transfers between devices: 19.7 us -> 9.85 us  [local(): lax.all_to_all(copies, 'tile', split_axis=0, concat_axis=0, tiled=True, a...]
    all_to_all x1, starting transfers between devices: 3.86 us -> 13.6 us  [local(): lax.all_to_all(frames.reshape(2 * channels, 8, 128), 'tile', split_axis=0...]
    all_to_all x1, waiting for transfers between devices: 13.5 us -> 3.79 us  [local(): lax.all_to_all(frames.reshape(2 * channels, 8, 128), 'tile', split_axis=0...]
    all_to_all x1, starting transfers between devices: 16.4 us -> 19.9 us  [local(): lax.all_to_all(copies, 'tile', split_axis=0, concat_axis=0, tiled=True, a...]
    all_gather x1, blocking collectives: 4.34 us -> 3.07 us  [local(): both = lax.all_gather(near, 'core', axis=0)]
    ppermute x1, starting transfers between devices: 1.92 us -> 3.19 us  [local(): from_far = lax.ppermute(far, TM, route)]
where the time goes in v2:
time: 62.7 us; the launch traced here: 62.3 us
  starting transfers between devices  36.7 us (59%)
  waiting for transfers between devices  15 us (24%)
  local copies, waits for them, and re-layouts  4.73 us (8%)
  blocking collectives  3.07 us (5%)
  Pallas kernels  2.07 us (3%)
  other arithmetic  0.66 us (1%)
    all_to_all x1, starting transfers between devices, local(): lax.all_to_all(copies, 'tile', split_axis=0, concat_axis=0, tiled=True, a...  19.9 us
    all_to_all x1, starting transfers between devices, local(): lax.all_to_all(frames.reshape(2 * channels, 8, 128), 'tile', split_axis=0...  13.6 us
    all_to_all x1, waiting for transfers between devices, local(): lax.all_to_all(copies, 'tile', split_axis=0, concat_axis=0, tiled=True, a...  9.85 us
    all_to_all x1, waiting for transfers between devices, local(): lax.all_to_all(frames.reshape(2 * channels, 8, 128), 'tile', split_axis=0...  3.79 us
    ppermute x1, starting transfers between devices, local(): from_far = lax.ppermute(far, TM, route)  3.19 us
    all_gather x1, blocking collectives, local(): both = lax.all_gather(near, 'core', axis=0)  3.07 us
    transpose x1, local copies, waits for them, and re-layouts, local(): jnp.transpose(conv_weight, (1, 2, 3, 0, 4))  1.81 us
    pallas_call x1, Pallas kernels, local(): pl.pallas_call(attend_kernel, out_shape=jax.ShapeDtypeStruct((CELLS, 4 *...  1.45 us
  transfers between devices with their start and end apart: 3, of which 3 were waited for; matrix products, arithmetic and copies ran while one was open for 4% of the time, Pallas kernels for 0%

profile of v2, /device:TPU:24, one launch (start us, length us, event | category | flops | bytes accessed | tf_op | source)
XLA Modules:
  0.0 62.3 jit_solution(411128669336674749)
XLA Ops:
  0.0 1.4 %broadcast_in_dim.11 = bf16[32,16,256]{2,1,0:T(8,128)(2,1)} broadcast(bf16[16,256]{1,0:T(8,128)(2,1)} %bitcast.17), dimensions={1,2} | broadcast | bytes 270336 | tf_op jit(solution)/shard_map/broadcast_in_dim | solution.py:105
  1.4 19.9 %all-to-all-start = ((bf16[32,16,256]{2,1,0:T(8,128)(2,1)}), bf16[32,16,256]{2,1,0:T(8,128)(2,1)S(1)}, u32[]{:S(2)}, u32[]{:S(2)}) async-start(bf16[32,16,256]{2,1,0:T(8,128)(2,1)} %broadcast_in_dim.11), calls=%async_computation | async-start | bytes 524288 | tf_op jit(solution)/shard_map/all_to_all | solution.py:107
  21.3 0.0 copy-start
  21.4 0.6 %copy-done = f32[16]{0:T(128)S(1)} copy-done((f32[16]{0:T(128)S(1)}, f32[16]{0:T(128)}, u32[]{:S(2)}) %copy-start) | copy-done | bytes 88
  22.0 0.1 copy.9.bias_ref
  22.1 1.8 %copy.8 = bf16[4,4,4,16,512]{4,3,2,1,0:T(8,128)(2,1)S(1)} copy(bf16[4,4,4,16,512]{4,2,1,0,3:T(4,128)(2,1)} %bitcast.16) | data formatting | bytes 2097152 | tf_op jit(solution)/shard_map/transpose | solution.py:108
  23.9 9.9 %all-to-all-done.latent_ref = bf16[32,16,256]{2,1,0:T(8,128)(2,1)S(1)} async-done(((bf16[32,16,256]{2,1,0:T(8,128)(2,1)}), bf16[32,16,256]{2,1,0:T(8,128)(2,1)S(1)}, u32[]{:S(2)}, u32[]{:S(2)}) %all-to-all-start) | async-done | bytes 262176 | tf_op jit(solution)/shard_map/all_to_all | solution.py:107
  33.7 0.6 %conv.1 = (f32[2,16,8,128]{3,2,1,0:T(8,128)S(1)}, bf16[16,8,128]{2,1,0:T(8,128)(2,1)S(1)}, bf16[16,8,128]{2,1,0:T(8,128)(2,1)S(1)}) custom-call(s32[1]{0:T(128)} %bitcast.core_ref, bf16[1024,512]{1,0:T(8,128)(2,1)S(1)} %bitcast.15, bf16[32,16,256]{2,1,0:T(8,128)(2,1)S(1)} %all-to-all-done.latent_ref, f32[16,1]{1,0:T(8,128)S(1)} %copy.9.bias_ref), custom_call_target="tpu_custom_call" | custom-call | tf_op jit(solution)/shard_map/conv/pallas_call | solution.py:114
  34.4 3.2 %collective-permute-start = (bf16[16,8,128]{2,1,0:T(8,128)(2,1)S(1)}, bf16[16,8,128]{2,1,0:T(8,128)(2,1)S(1)}, u32[]{:S(2)}, u32[]{:S(2)}) collective-permute-start(bf16[16,8,128]{2,1,0:T(8,128)(2,1)S(1)} %get-tuple-element.9), channel_id=1, source_target_pairs={{32,64},{96,128},{160,192},{224,256},{288,320},{352,384},{416,448}... | collective-permute-start | bytes 98312 | tf_op jit(solution)/shard_map/ppermute | solution.py:126
  37.6 3.1 %all-gather = bf16[32,8,128]{2,1,0:T(8,128)(2,1)S(1)} all-gather(bf16[16,8,128]{2,1,0:T(8,128)(2,1)S(1)} %get-tuple-element.10), channel_id=2, replica_groups=mesh['pair'=8,'core'=2,'tile'=32] {'core'}, dimensions={0}, use_global_device_ids=true | all-gather | bytes 98304 | tf_op jit(solution)/shard_map/all_gather | solution.py:127
  40.7 1.4 %collective-permute-done = bf16[16,8,128]{2,1,0:T(8,128)(2,1)S(1)} collective-permute-done((bf16[16,8,128]{2,1,0:T(8,128)(2,1)S(1)}, bf16[16,8,128]{2,1,0:T(8,128)(2,1)S(1)}, u32[]{:S(2)}, u32[]{:S(2)}) %collective-permute-start) | collective-permute-done | bytes 32800 | tf_op jit(solution)/shard_map/ppermute | solution.py:126
  42.0 0.6 %add_convert_fusion = bf16[2,16,8,128]{3,2,1,0:T(8,128)(2,1)} fusion(f32[2,16,8,128]{3,2,1,0:T(8,128)S(1)} %get-tuple-element.8, bf16[1,16,8,128]{3,2,1,0:T(8,128)(2,1)S(1)} %get-tuple-element.12, bf16[1,16,8,128]{3,2,1,0:T(8,128)(2,1)S(1)} %get-tuple-element.11), kind=kLoop, calls=%fused_computation | loop fusion | flops 131072 | bytes 262144 | tf_op jit(solution)/shard_map/convert_element_type | solution.py:131
  42.7 13.6 %all-to-all-start.1 = ((bf16[32,8,128]{2,1,0:T(8,128)(2,1)}), bf16[32,8,128]{2,1,0:T(8,128)(2,1)S(1)}, u32[]{:S(2)}, u32[]{:S(2)}) async-start(bf16[32,8,128]{2,1,0:T(8,128)(2,1)} %bitcast.7), calls=%async_computation.1 | async-start | bytes 131072 | tf_op jit(solution)/shard_map/all_to_all | solution.py:132
  56.3 0.8 %dynamic-slice_bitcast_fusion = (bf16[128,128]{1,0:T(8,128)(2,1)S(1)}, bf16[128,128]{1,0:T(8,128)(2,1)S(1)}) fusion(bf16[16,128,128]{2,1,0:T(8,128)(2,1)} %param.9, s32[]{:T(128)S(6)} %select_n.40, bf16[16,128,128]{2,1,0:T(8,128)(2,1)} %param.8), kind=kLoop, calls=%fused_computation.2 | loop fusion | bytes 131076 | tf_op jit(solution)/shard_map/jit(dynamic_index_in_dim)/squeeze | solution.py:111
  57.1 3.8 %all-to-all-done.1.piece_ref = bf16[32,8,128]{2,1,0:T(8,128)(2,1)S(1)} async-done(((bf16[32,8,128]{2,1,0:T(8,128)(2,1)}), bf16[32,8,128]{2,1,0:T(8,128)(2,1)S(1)}, u32[]{:S(2)}, u32[]{:S(2)}) %all-to-all-start.1) | async-done | bytes 65568 | tf_op jit(solution)/shard_map/all_to_all | solution.py:132
  60.9 1.4 %attend.1 = bf16[256,128]{1,0:T(8,128)(2,1)} custom-call(bf16[32,8,128]{2,1,0:T(8,128)(2,1)S(1)} %all-to-all-done.1.piece_ref, bf16[128,128]{1,0:T(8,128)(2,1)S(1)} %get-tuple-element.14.query_ref, bf16[128,128]{1,0:T(8,128)(2,1)S(1)} %get-tuple-element.13.key_ref), custom_call_target="tpu_custom_call" | custom-call | tf_op jit(solution)/shard_map/attend/pallas_call | solution.py:136
  (1 shorter events, 0.0 us)
Async XLA Ops:
  1.4 32.3 %all-to-all-start = ((bf16[32,16,256]{2,1,0:T(8,128)(2,1)}), bf16[32,16,256]{2,1,0:T(8,128)(2,1)S(1)}, u32[]{:S(2)}, u32[]{:S(2)}) async-start(bf16[32,16,256]{2,1,0:T(8,128)(2,1)} %broadcast_in_dim.11), calls=%async_computation | async-start | bytes 524288 | tf_op jit(solution)/shard_map/all_to_all | solution.py:107
  21.3 0.7 %copy-start = (f32[16]{0:T(128)S(1)}, f32[16]{0:T(128)}, u32[]{:S(2)}) copy-start(f32[16]{0:T(128)} %param.7) | copy-start | bytes 196
  34.4 7.6 %collective-permute-start = (bf16[16,8,128]{2,1,0:T(8,128)(2,1)S(1)}, bf16[16,8,128]{2,1,0:T(8,128)(2,1)S(1)}, u32[]{:S(2)}, u32[]{:S(2)}) collective-permute-start(bf16[16,8,128]{2,1,0:T(8,128)(2,1)S(1)} %get-tuple-element.9), channel_id=1, source_target_pairs={{32,64},{96,128},{160,192},{224,256},{288,320},{352,384},{416,448}... | collective-permute-start | bytes 98312 | tf_op jit(solution)/shard_map/ppermute | solution.py:126
  42.7 18.2 %all-to-all-start.1 = ((bf16[32,8,128]{2,1,0:T(8,128)(2,1)}), bf16[32,8,128]{2,1,0:T(8,128)(2,1)S(1)}, u32[]{:S(2)}, u32[]{:S(2)}) async-start(bf16[32,8,128]{2,1,0:T(8,128)(2,1)} %bitcast.7), calls=%async_computation.1 | async-start | bytes 131072 | tf_op jit(solution)/shard_map/all_to_all | solution.py:132

commit v3 on v2

--- a/solution.py
+++ b/solution.py
@@ -9,6 +9,7 @@
 SIDE = 16
 CELLS = SIDE * SIDE
 TM = ("pair", "core")
+TILE = ("xl", "z")
 VMEM_LIMIT = 32 * 1024 * 1024
 
 
@@ -99,14 +100,18 @@
 
 
 def local(latent, conv_weight, conv_bias, query_weight, key_weight):
-    tiles = lax.axis_size("tile")
+    tiles = lax.axis_size(TILE)
     channels = conv_weight.shape[0]
     core = lax.axis_index("core").astype(jnp.int32)
-    copies = jnp.broadcast_to(latent, (tiles,) + latent.shape[1:])
+    depth = lax.axis_size("z")
     order, _ = turned(tiles)
-    gathered = lax.all_to_all(copies, "tile", split_axis=0, concat_axis=0, tiled=True, axis_index_groups=[order])
+    copies = jnp.broadcast_to(latent, (depth,) + latent.shape[1:])
+    column = lax.all_to_all(
+        copies, "z", split_axis=0, concat_axis=0, tiled=True, axis_index_groups=[order[:depth]]
+    )
+    gathered = lax.all_gather(column, "xl", axis=0, tiled=True)
     rows = jnp.transpose(conv_weight, (1, 2, 3, 0, 4)).reshape(-1, conv_weight.shape[-1])
-    head = lax.axis_index("tile") % HEADS
+    head = lax.axis_index(TILE) % HEADS
     query_rows = lax.dynamic_index_in_dim(query_weight, head, 0, keepdims=False)
     key_rows = lax.dynamic_index_in_dim(key_weight, head, 0, keepdims=False)
 
@@ -130,7 +135,7 @@
     to_second = jnp.where(core == 0, from_near, from_far).astype(jnp.float32)
     frames = (own + jnp.stack([to_first, to_second])).astype(jnp.bfloat16)
     received = lax.all_to_all(
-        frames.reshape(2 * channels, 8, 128), "tile", split_axis=0, concat_axis=0, tiled=True, axis_index_groups=[order]
+        frames.reshape(2 * channels, 8, 128), TILE, split_axis=0, concat_axis=0, tiled=True, axis_index_groups=[order]
     )
     vmem = pl.BlockSpec(memory_space=pltpu.VMEM)
     attended = pl.pallas_call(
@@ -146,7 +151,7 @@
 
 
 def solution(mesh):
-    split = Mesh(mesh.devices.reshape(-1, 2, mesh.devices.shape[1]), ("pair", "core", "tile"))
-    in_specs = (P(TM, "tile", None), P("tile", None, None, None, None), P("tile"), P(), P())
-    out_specs = P(TM + ("tile",), None, None)
+    split = Mesh(mesh.devices.reshape(-1, 2, 2, mesh.devices.shape[1] // 2), TM + TILE)
+    in_specs = (P(TM, TILE, None), P(TILE, None, None, None, None), P(TILE), P(), P())
+    out_specs = P(TM + TILE, None, None)
     return jax.shard_map(local, mesh=split, in_specs=in_specs, out_specs=out_specs, check_vma=False)

time: 62.7 us -> 60.8 us (0.970)
  blocking collectives: 3.07 us -> 9.39 us
  waiting for transfers between devices: 15 us -> 8.74 us
  starting transfers between devices: 36.7 us -> 34.7 us
    all_to_all x2, waiting for transfers between devices: 13.6 us -> 7.67 us  [the longest x1 3.96 us: local(): lax.all_to_all(copies, 'z', split_axis=0, concat_axis=0, tiled=True, axis...]
    all_gather x0 -> x1, blocking collectives: none -> 5.63 us  [local(): gathered = lax.all_gather(column, 'xl', axis=0, tiled=True)]
    all_to_all x2, starting transfers between devices: 33.5 us -> 32 us  [the longest x1 18.9 us: local(): lax.all_to_all(copies, 'z', split_axis=0, concat_axis=0, tiled=True, axis...]
    all_gather x1, blocking collectives: 3.07 us -> 3.76 us  [local(): both = lax.all_gather(near, 'core', axis=0)]
where the time goes in v3:
time: 60.8 us; the launch traced here: 60.4 us
  starting transfers between devices  34.7 us (57%)
  blocking collectives  9.39 us (15%)
  waiting for transfers between devices  8.74 us (14%)
  local copies, waits for them, and re-layouts  4.68 us (8%)
  Pallas kernels  2.08 us (3%)
  other arithmetic  0.66 us (1%)
    all_to_all x1, starting transfers between devices, local(): lax.all_to_all(copies, 'z', split_axis=0, concat_axis=0, tiled=True, axis...  18.9 us
    all_to_all x1, starting transfers between devices, local(): lax.all_to_all(frames.reshape(2 * channels, 8, 128), TILE, split_axis=0,...  13.1 us
    all_gather x1, blocking collectives, local(): gathered = lax.all_gather(column, 'xl', axis=0, tiled=True)  5.63 us
    all_to_all x1, waiting for transfers between devices, local(): lax.all_to_all(copies, 'z', split_axis=0, concat_axis=0, tiled=True, axis...  3.96 us
    all_gather x1, blocking collectives, local(): both = lax.all_gather(near, 'core', axis=0)  3.76 us
    all_to_all x1, waiting for transfers between devices, local(): lax.all_to_all(frames.reshape(2 * channels, 8, 128), TILE, split_axis=0,...  3.72 us
    ppermute x1, starting transfers between devices, local(): from_far = lax.ppermute(far, TM, route)  2.8 us
    transpose x1, local copies, waits for them, and re-layouts, local(): jnp.transpose(conv_weight, (1, 2, 3, 0, 4))  1.81 us
  transfers between devices with their start and end apart: 3, of which 3 were waited for; matrix products, arithmetic and copies ran while one was open for 4% of the time, Pallas kernels for 0%

profile of v3, /device:TPU:24, one launch (start us, length us, event | category | flops | bytes accessed | tf_op | source)
XLA Modules:
  0.0 60.4 jit_solution(17703142689322756932)
XLA Ops:
  0.0 1.4 %broadcast_in_dim.11 = bf16[16,16,256]{2,1,0:T(8,128)(2,1)} broadcast(bf16[16,256]{1,0:T(8,128)(2,1)} %bitcast.17), dimensions={1,2} | broadcast | bytes 139264 | tf_op jit(solution)/shard_map/broadcast_in_dim | solution.py:108
  1.4 18.9 %all-to-all-start = ((bf16[16,16,256]{2,1,0:T(8,128)(2,1)}), bf16[16,16,256]{2,1,0:T(8,128)(2,1)S(1)}, u32[]{:S(2)}, u32[]{:S(2)}) async-start(bf16[16,16,256]{2,1,0:T(8,128)(2,1)} %broadcast_in_dim.11), calls=%async_computation | async-start | bytes 262144 | tf_op jit(solution)/shard_map/all_to_all | solution.py:109
  20.2 1.8 %copy.8 = bf16[4,4,4,16,512]{4,3,2,1,0:T(8,128)(2,1)S(1)} copy(bf16[4,4,4,16,512]{4,2,1,0,3:T(4,128)(2,1)} %bitcast.16) | data formatting | bytes 2097152 | tf_op jit(solution)/shard_map/transpose | solution.py:113
  22.0 0.0 copy-start
  22.0 0.6 %copy-done = f32[16]{0:T(128)S(1)} copy-done((f32[16]{0:T(128)S(1)}, f32[16]{0:T(128)}, u32[]{:S(2)}) %copy-start) | copy-done | bytes 88
  22.7 0.1 copy.9.bias_ref
  22.8 4.0 %all-to-all-done = bf16[16,16,256]{2,1,0:T(8,128)(2,1)S(1)} async-done(((bf16[16,16,256]{2,1,0:T(8,128)(2,1)}), bf16[16,16,256]{2,1,0:T(8,128)(2,1)S(1)}, u32[]{:S(2)}, u32[]{:S(2)}) %all-to-all-start) | async-done | bytes 131104 | tf_op jit(solution)/shard_map/all_to_all | solution.py:109
  26.7 5.6 %all_gather.9.latent_ref = bf16[32,16,256]{2,1,0:T(8,128)(2,1)S(1)} all-gather(bf16[16,16,256]{2,1,0:T(8,128)(2,1)S(1)} %all-to-all-done), channel_id=1, replica_groups=mesh['pair'=8,'core'=2,'xl'=2,'z'=16] {'xl'}, dimensions={0}, use_global_device_ids=true | all-gather | bytes 393216 | tf_op jit(solution)/shard_map/all_gather | solution.py:112
  32.3 0.6 %conv.1 = (f32[2,16,8,128]{3,2,1,0:T(8,128)S(1)}, bf16[16,8,128]{2,1,0:T(8,128)(2,1)S(1)}, bf16[16,8,128]{2,1,0:T(8,128)(2,1)S(1)}) custom-call(s32[1]{0:T(128)} %bitcast.core_ref, bf16[1024,512]{1,0:T(8,128)(2,1)S(1)} %bitcast.15, bf16[32,16,256]{2,1,0:T(8,128)(2,1)S(1)} %all_gather.9.latent_ref, f32[16,1]{1,0:T(8,128)S(1)} %copy.9.bias_ref), custom_call_target="tpu_custom_call" | custom-call | tf_op jit(solution)/shard_map/conv/pallas_call | solution.py:119
  33.0 2.8 %collective-permute-start = (bf16[16,8,128]{2,1,0:T(8,128)(2,1)S(1)}, bf16[16,8,128]{2,1,0:T(8,128)(2,1)S(1)}, u32[]{:S(2)}, u32[]{:S(2)}) collective-permute-start(bf16[16,8,128]{2,1,0:T(8,128)(2,1)S(1)} %get-tuple-element.9), channel_id=1, source_target_pairs={{32,64},{96,128},{160,192},{224,256},{288,320},{352,384},{416,448}... | collective-permute-start | bytes 98312 | tf_op jit(solution)/shard_map/ppermute | solution.py:131
  35.8 3.8 %all-gather = bf16[32,8,128]{2,1,0:T(8,128)(2,1)S(1)} all-gather(bf16[16,8,128]{2,1,0:T(8,128)(2,1)S(1)} %get-tuple-element.10), channel_id=2, replica_groups=mesh['pair'=8,'core'=2,'xl'=2,'z'=16] {'core'}, dimensions={0}, use_global_device_ids=true | all-gather | bytes 98304 | tf_op jit(solution)/shard_map/all_gather | solution.py:132
  39.6 1.1 %collective-permute-done = bf16[16,8,128]{2,1,0:T(8,128)(2,1)S(1)} collective-permute-done((bf16[16,8,128]{2,1,0:T(8,128)(2,1)S(1)}, bf16[16,8,128]{2,1,0:T(8,128)(2,1)S(1)}, u32[]{:S(2)}, u32[]{:S(2)}) %collective-permute-start) | collective-permute-done | bytes 32800 | tf_op jit(solution)/shard_map/ppermute | solution.py:131
  40.6 0.6 %add_convert_fusion = bf16[2,16,8,128]{3,2,1,0:T(8,128)(2,1)} fusion(f32[2,16,8,128]{3,2,1,0:T(8,128)S(1)} %get-tuple-element.8, bf16[1,16,8,128]{3,2,1,0:T(8,128)(2,1)S(1)} %get-tuple-element.12, bf16[1,16,8,128]{3,2,1,0:T(8,128)(2,1)S(1)} %get-tuple-element.11), kind=kLoop, calls=%fused_computation | loop fusion | flops 131072 | bytes 262144 | tf_op jit(solution)/shard_map/convert_element_type | solution.py:136
  41.3 13.1 %all-to-all-start.1 = ((bf16[32,8,128]{2,1,0:T(8,128)(2,1)}), bf16[32,8,128]{2,1,0:T(8,128)(2,1)S(1)}, u32[]{:S(2)}, u32[]{:S(2)}) async-start(bf16[32,8,128]{2,1,0:T(8,128)(2,1)} %bitcast.7), calls=%async_computation.1 | async-start | bytes 131072 | tf_op jit(solution)/shard_map/all_to_all | solution.py:137
  54.4 0.8 %dynamic-slice_bitcast_fusion = (bf16[128,128]{1,0:T(8,128)(2,1)S(1)}, bf16[128,128]{1,0:T(8,128)(2,1)S(1)}) fusion(bf16[16,128,128]{2,1,0:T(8,128)(2,1)} %param.9, s32[]{:T(128)S(6)} %select_n.40, bf16[16,128,128]{2,1,0:T(8,128)(2,1)} %param.8), kind=kLoop, calls=%fused_computation.2 | loop fusion | bytes 131076 | tf_op jit(solution)/shard_map/jit(dynamic_index_in_dim)/squeeze | solution.py:116
  55.2 3.7 %all-to-all-done.1.piece_ref = bf16[32,8,128]{2,1,0:T(8,128)(2,1)S(1)} async-done(((bf16[32,8,128]{2,1,0:T(8,128)(2,1)}), bf16[32,8,128]{2,1,0:T(8,128)(2,1)S(1)}, u32[]{:S(2)}, u32[]{:S(2)}) %all-to-all-start.1) | async-done | bytes 65568 | tf_op jit(solution)/shard_map/all_to_all | solution.py:137
  58.9 1.5 %attend.1 = bf16[256,128]{1,0:T(8,128)(2,1)} custom-call(bf16[32,8,128]{2,1,0:T(8,128)(2,1)S(1)} %all-to-all-done.1.piece_ref, bf16[128,128]{1,0:T(8,128)(2,1)S(1)} %get-tuple-element.14.query_ref, bf16[128,128]{1,0:T(8,128)(2,1)S(1)} %get-tuple-element.13.key_ref), custom_call_target="tpu_custom_call" | custom-call | tf_op jit(solution)/shard_map/attend/pallas_call | solution.py:141
  (1 shorter events, 0.0 us)
Async XLA Ops:
  1.4 25.4 %all-to-all-start = ((bf16[16,16,256]{2,1,0:T(8,128)(2,1)}), bf16[16,16,256]{2,1,0:T(8,128)(2,1)S(1)}, u32[]{:S(2)}, u32[]{:S(2)}) async-start(bf16[16,16,256]{2,1,0:T(8,128)(2,1)} %broadcast_in_dim.11), calls=%async_computation | async-start | bytes 262144 | tf_op jit(solution)/shard_map/all_to_all | solution.py:109
  22.0 0.7 %copy-start = (f32[16]{0:T(128)S(1)}, f32[16]{0:T(128)}, u32[]{:S(2)}) copy-start(f32[16]{0:T(128)} %param.7) | copy-start | bytes 196
  33.0 7.6 %collective-permute-start = (bf16[16,8,128]{2,1,0:T(8,128)(2,1)S(1)}, bf16[16,8,128]{2,1,0:T(8,128)(2,1)S(1)}, u32[]{:S(2)}, u32[]{:S(2)}) collective-permute-start(bf16[16,8,128]{2,1,0:T(8,128)(2,1)S(1)} %get-tuple-element.9), channel_id=1, source_target_pairs={{32,64},{96,128},{160,192},{224,256},{288,320},{352,384},{416,448}... | collective-permute-start | bytes 98312 | tf_op jit(solution)/shard_map/ppermute | solution.py:131
  41.3 17.6 %all-to-all-start.1 = ((bf16[32,8,128]{2,1,0:T(8,128)(2,1)}), bf16[32,8,128]{2,1,0:T(8,128)(2,1)S(1)}, u32[]{:S(2)}, u32[]{:S(2)}) async-start(bf16[32,8,128]{2,1,0:T(8,128)(2,1)} %bitcast.7), calls=%async_computation.1 | async-start | bytes 131072 | tf_op jit(solution)/shard_map/all_to_all | solution.py:137

commit v4 on v3

--- a/solution.py
+++ b/solution.py
@@ -13,9 +13,12 @@
 VMEM_LIMIT = 32 * 1024 * 1024
 
 
-def turned(order):
+FIRST_GATHER, FIRST_FRAMES = 8, 8
+
+
+def turned(order, first):
     half = order // 2
-    tiles = [start + (z + half // 2) % half for start in (0, half) for z in range(half)]
+    tiles = [start + (z + first) % half for start in (0, half) for z in range(half)]
     return tiles, [tiles.index(tile) for tile in range(order)]
 
 
@@ -44,7 +47,7 @@
 def conv_kernel(core_ref, weight_ref, latent_ref, bias_ref, own_ref, near_ref, far_ref, later_ref, earlier_ref):
     channels = bias_ref.shape[0]
     rows = 16 * channels
-    _, places = turned(latent_ref.shape[0])
+    _, places = turned(latent_ref.shape[0], FIRST_GATHER)
     latent = in_turn(latent_ref, places)
     for kt in (3, 0, 1, 2):
         products = jnp.dot(
@@ -66,13 +69,11 @@
                 elif kt == 0:
                     earlier_ref[:, place, :] = piece
                 else:
-                    middle = channels // 2
-                    own_ref[kt - 1, :middle, place, :] = piece[middle:]
-                    own_ref[kt - 1, middle:, place, :] = piece[:middle]
+                    own_ref[kt - 1, : channels - FIRST_FRAMES, place, :] = piece[FIRST_FRAMES:]
+                    own_ref[kt - 1, channels - FIRST_FRAMES :, place, :] = piece[:FIRST_FRAMES]
     first = core_ref[0] == 0
-    middle = channels // 2
-    later = jnp.concatenate([later_ref[middle:], later_ref[:middle]], 0)
-    earlier = jnp.concatenate([earlier_ref[middle:], earlier_ref[:middle]], 0)
+    later = jnp.concatenate([later_ref[FIRST_FRAMES:], later_ref[:FIRST_FRAMES]], 0)
+    earlier = jnp.concatenate([earlier_ref[FIRST_FRAMES:], earlier_ref[:FIRST_FRAMES]], 0)
     near_ref[...] = jnp.where(first, later, earlier).astype(jnp.bfloat16)
     far_ref[...] = jnp.where(first, earlier, later).astype(jnp.bfloat16)
 
@@ -80,13 +81,19 @@
 def attend_kernel(piece_ref, query_ref, key_ref, out_ref, wide_ref, turned_ref):
     wide_ref[...] = piece_ref[...].astype(jnp.float32)
     channels = wide_ref.shape[0]
-    tiles, _ = turned(channels)
+    column = channels // 2
+    runs = [
+        (start + skip, start + (skip + FIRST_FRAMES) % column, size)
+        for start in (0, column)
+        for skip, size in ((0, column - FIRST_FRAMES), (column - FIRST_FRAMES, FIRST_FRAMES))
+        if size
+    ]
     for place in range(8):
         parity, half = place // 2, place % 2
         columns = slice(half * 128, (half + 1) * 128)
-        for run in range(0, channels, 8):
-            start = parity * channels + tiles[run]
-            turned_ref[start : start + 8, columns] = wide_ref[run : run + 8, place, :]
+        for source, target, size in runs:
+            start = parity * channels + target
+            turned_ref[start : start + size, columns] = wide_ref[source : source + size, place, :]
     wide = turned_ref[...].T
     tokens = wide.astype(jnp.bfloat16)
     queries = jnp.dot(tokens, query_ref[...], preferred_element_type=jnp.float32).astype(jnp.bfloat16)
@@ -104,16 +111,19 @@
     channels = conv_weight.shape[0]
     core = lax.axis_index("core").astype(jnp.int32)
     depth = lax.axis_size("z")
-    order, _ = turned(tiles)
+    gather_order, _ = turned(tiles, FIRST_GATHER)
+    frames_order, _ = turned(tiles, FIRST_FRAMES)
     copies = jnp.broadcast_to(latent, (depth,) + latent.shape[1:])
     column = lax.all_to_all(
-        copies, "z", split_axis=0, concat_axis=0, tiled=True, axis_index_groups=[order[:depth]]
+        copies, "z", split_axis=0, concat_axis=0, tiled=True, axis_index_groups=[gather_order[:depth]]
     )
     gathered = lax.all_gather(column, "xl", axis=0, tiled=True)
     rows = jnp.transpose(conv_weight, (1, 2, 3, 0, 4)).reshape(-1, conv_weight.shape[-1])
     head = lax.axis_index(TILE) % HEADS
     query_rows = lax.dynamic_index_in_dim(query_weight, head, 0, keepdims=False)
     key_rows = lax.dynamic_index_in_dim(key_weight, head, 0, keepdims=False)
+
+    rows, query_rows, key_rows = lax.optimization_barrier((rows, query_rows, key_rows))
 
     edge = jax.ShapeDtypeStruct((channels, 8, 128), jnp.bfloat16)
     own, near, far = pl.pallas_call(
@@ -135,7 +145,7 @@
     to_second = jnp.where(core == 0, from_near, from_far).astype(jnp.float32)
     frames = (own + jnp.stack([to_first, to_second])).astype(jnp.bfloat16)
     received = lax.all_to_all(
-        frames.reshape(2 * channels, 8, 128), TILE, split_axis=0, concat_axis=0, tiled=True, axis_index_groups=[order]
+        frames.reshape(2 * channels, 8, 128), TILE, split_axis=0, concat_axis=0, tiled=True, axis_index_groups=[frames_order]
     )
     vmem = pl.BlockSpec(memory_space=pltpu.VMEM)
     attended = pl.pallas_call(

time: 60.8 us -> 59.9 us (0.985)
  blocking collectives: 9.39 us -> 26.8 us
  starting transfers between devices: 34.7 us -> 21.6 us
  waiting for transfers between devices: 8.74 us -> 4.24 us
  other arithmetic: 0.66 us -> 0.03 us
    all_to_all x0 -> x1, blocking collectives: none -> 17.4 us  [local(): lax.all_to_all(frames.reshape(2 * channels, 8, 128), TILE, split_axis=0,...]
    all_to_all x1 -> x0, starting transfers between devices: 13.1 us -> none  [local(): lax.all_to_all(frames.reshape(2 * channels, 8, 128), TILE, split_axis=0,...]
    all_to_all x1 -> x0, waiting for transfers between devices: 3.72 us -> none  [local(): lax.all_to_all(frames.reshape(2 * channels, 8, 128), TILE, split_axis=0,...]
    all_to_all x1, waiting for transfers between devices: 3.96 us -> 3.17 us  [local(): lax.all_to_all(copies, 'z', split_axis=0, concat_axis=0, tiled=True, axis...]
    convert_element_type x1, other arithmetic: 0.65 us -> 0.02 us  [local(): frames = (own + jnp.stack([to_first, to_second])).astype(jnp.bfloat16)]
  transfers between devices with their start and end apart: 3 -> 2, of which waited for: 3 -> 2; matrix products, arithmetic and copies ran while one was open for 4% -> 4% of each run, Pallas kernels for 0% -> 0%
where the time goes in v4:
time: 59.9 us; the launch traced here: 59.5 us
  blocking collectives  26.8 us (45%)
  starting transfers between devices  21.6 us (36%)
  local copies, waits for them, and re-layouts  4.68 us (8%)
  waiting for transfers between devices  4.24 us (7%)
  Pallas kernels  2.08 us (3%)
    all_to_all x1, starting transfers between devices, local(): lax.all_to_all(copies, 'z', split_axis=0, concat_axis=0, tiled=True, axis...  18.9 us
    all_to_all x1, blocking collectives, local(): lax.all_to_all(frames.reshape(2 * channels, 8, 128), TILE, split_axis=0,...  17.4 us
    all_gather x1, blocking collectives, local(): gathered = lax.all_gather(column, 'xl', axis=0, tiled=True)  5.63 us
    all_gather x1, blocking collectives, local(): both = lax.all_gather(near, 'core', axis=0)  3.76 us
    all_to_all x1, waiting for transfers between devices, local(): lax.all_to_all(copies, 'z', split_axis=0, concat_axis=0, tiled=True, axis...  3.17 us
    ppermute x1, starting transfers between devices, local(): from_far = lax.ppermute(far, TM, route)  2.79 us
    transpose x1, local copies, waits for them, and re-layouts, local(): jnp.transpose(conv_weight, (1, 2, 3, 0, 4))  1.81 us
    pallas_call x1, Pallas kernels, local(): pl.pallas_call(attend_kernel, out_shape=jax.ShapeDtypeStruct((CELLS, 4 *...  1.45 us
  transfers between devices with their start and end apart: 2, of which 2 were waited for; matrix products, arithmetic and copies ran while one was open for 4% of the time, Pallas kernels for 0%

profile of v4, /device:TPU:24, one launch (start us, length us, event | category | flops | bytes accessed | tf_op | source)
XLA Modules:
  0.0 59.5 jit_solution(2556872507546904511)
XLA Ops:
  0.0 1.4 %broadcast_in_dim.11 = bf16[16,16,256]{2,1,0:T(8,128)(2,1)} broadcast(bf16[16,256]{1,0:T(8,128)(2,1)} %bitcast.18), dimensions={1,2} | broadcast | bytes 139264 | tf_op jit(solution)/shard_map/broadcast_in_dim | solution.py:116
  1.4 18.9 %all-to-all-start = ((bf16[16,16,256]{2,1,0:T(8,128)(2,1)}), bf16[16,16,256]{2,1,0:T(8,128)(2,1)S(1)}, u32[]{:S(2)}, u32[]{:S(2)}) async-start(bf16[16,16,256]{2,1,0:T(8,128)(2,1)} %broadcast_in_dim.11), calls=%async_computation | async-start | bytes 262144 | tf_op jit(solution)/shard_map/all_to_all | solution.py:117
  20.2 1.8 %copy.8 = bf16[4,4,4,16,512]{4,3,2,1,0:T(8,128)(2,1)S(1)} copy(bf16[4,4,4,16,512]{4,2,1,0,3:T(4,128)(2,1)} %bitcast.16) | data formatting | bytes 2097152 | tf_op jit(solution)/shard_map/transpose | solution.py:121
  22.0 0.8 %dynamic-slice_bitcast_fusion = (bf16[128,128]{1,0:T(8,128)(2,1)S(1)}, bf16[128,128]{1,0:T(8,128)(2,1)S(1)}) fusion(bf16[16,128,128]{2,1,0:T(8,128)(2,1)} %param.9, s32[]{:T(128)S(6)} %select_n.34, bf16[16,128,128]{2,1,0:T(8,128)(2,1)} %param.8), kind=kLoop, calls=%fused_computation.4 | loop fusion | bytes 131076 | tf_op jit(solution)/shard_map/jit(dynamic_index_in_dim)/squeeze | solution.py:124
  22.8 0.0 copy-start
  22.8 0.7 %copy-done = f32[16]{0:T(128)S(1)} copy-done((f32[16]{0:T(128)S(1)}, f32[16]{0:T(128)}, u32[]{:S(2)}) %copy-start) | copy-done | bytes 88
  23.5 0.1 copy.9.bias_ref
  23.5 3.2 %all-to-all-done = bf16[16,16,256]{2,1,0:T(8,128)(2,1)S(1)} async-done(((bf16[16,16,256]{2,1,0:T(8,128)(2,1)}), bf16[16,16,256]{2,1,0:T(8,128)(2,1)S(1)}, u32[]{:S(2)}, u32[]{:S(2)}) %all-to-all-start) | async-done | bytes 131104 | tf_op jit(solution)/shard_map/all_to_all | solution.py:117
  26.7 5.6 %all_gather.9.latent_ref = bf16[32,16,256]{2,1,0:T(8,128)(2,1)S(1)} all-gather(bf16[16,16,256]{2,1,0:T(8,128)(2,1)S(1)} %all-to-all-done), channel_id=1, replica_groups=mesh['pair'=8,'core'=2,'xl'=2,'z'=16] {'xl'}, dimensions={0}, use_global_device_ids=true | all-gather | bytes 393216 | tf_op jit(solution)/shard_map/all_gather | solution.py:120
  32.3 0.6 %conv.1 = (f32[2,16,8,128]{3,2,1,0:T(8,128)S(1)}, bf16[16,8,128]{2,1,0:T(8,128)(2,1)S(1)}, bf16[16,8,128]{2,1,0:T(8,128)(2,1)S(1)}) custom-call(s32[1]{0:T(128)} %bitcast.core_ref, bf16[1024,512]{1,0:T(8,128)(2,1)S(1)} %bitcast.15, bf16[32,16,256]{2,1,0:T(8,128)(2,1)S(1)} %all_gather.9.latent_ref, f32[16,1]{1,0:T(8,128)S(1)} %copy.9.bias_ref), custom_call_target="tpu_custom_call" | custom-call | tf_op jit(solution)/shard_map/conv/pallas_call | solution.py:129
  33.0 2.8 %collective-permute-start = (bf16[16,8,128]{2,1,0:T(8,128)(2,1)S(1)}, bf16[16,8,128]{2,1,0:T(8,128)(2,1)S(1)}, u32[]{:S(2)}, u32[]{:S(2)}) collective-permute-start(bf16[16,8,128]{2,1,0:T(8,128)(2,1)S(1)} %get-tuple-element.13), channel_id=1, source_target_pairs={{32,64},{96,128},{160,192},{224,256},{288,320},{352,384},{416,448}... | collective-permute-start | bytes 98312 | tf_op jit(solution)/shard_map/ppermute | solution.py:141
  35.8 3.8 %all-gather = bf16[32,8,128]{2,1,0:T(8,128)(2,1)S(1)} all-gather(bf16[16,8,128]{2,1,0:T(8,128)(2,1)S(1)} %get-tuple-element.14), channel_id=2, replica_groups=mesh['pair'=8,'core'=2,'xl'=2,'z'=16] {'core'}, dimensions={0}, use_global_device_ids=true | all-gather | bytes 98304 | tf_op jit(solution)/shard_map/all_gather | solution.py:142
  39.5 1.1 %collective-permute-done = bf16[16,8,128]{2,1,0:T(8,128)(2,1)S(1)} collective-permute-done((bf16[16,8,128]{2,1,0:T(8,128)(2,1)S(1)}, bf16[16,8,128]{2,1,0:T(8,128)(2,1)S(1)}, u32[]{:S(2)}, u32[]{:S(2)}) %collective-permute-start) | collective-permute-done | bytes 32800 | tf_op jit(solution)/shard_map/ppermute | solution.py:141
  40.7 17.4 %all_to_all.10.piece_ref = bf16[32,8,128]{2,1,0:T(8,128)(2,1)S(1)} all-to-all(bf16[32,8,128]{2,1,0:T(8,128)(2,1)S(1)} %bitcast.17), channel_id=1, replica_groups={{8,9,10,11,12,13,14,15,0,1,2,3,4,5,6,7,24,25,26,27,28,29,30,31,16,17,18..., dimensions={0} | all-to-all | bytes 131072 | tf_op jit(solution)/shard_map/all_to_all | solution.py:147
  58.1 1.5 %attend.1 = bf16[256,128]{1,0:T(8,128)(2,1)} custom-call(bf16[32,8,128]{2,1,0:T(8,128)(2,1)S(1)} %all_to_all.10.piece_ref, bf16[128,128]{1,0:T(8,128)(2,1)S(1)} %get-tuple-element.15.query_ref, bf16[128,128]{1,0:T(8,128)(2,1)S(1)} %get-tuple-element.16.key_ref), custom_call_target="tpu_custom_call" | custom-call | tf_op jit(solution)/shard_map/attend/pallas_call | solution.py:151
  (2 shorter events, 0.0 us)
Async XLA Ops:
  1.4 25.4 %all-to-all-start = ((bf16[16,16,256]{2,1,0:T(8,128)(2,1)}), bf16[16,16,256]{2,1,0:T(8,128)(2,1)S(1)}, u32[]{:S(2)}, u32[]{:S(2)}) async-start(bf16[16,16,256]{2,1,0:T(8,128)(2,1)} %broadcast_in_dim.11), calls=%async_computation | async-start | bytes 262144 | tf_op jit(solution)/shard_map/all_to_all | solution.py:117
  22.8 0.7 %copy-start = (f32[16]{0:T(128)S(1)}, f32[16]{0:T(128)}, u32[]{:S(2)}) copy-start(f32[16]{0:T(128)} %param.7) | copy-start | bytes 196
  33.0 7.6 %collective-permute-start = (bf16[16,8,128]{2,1,0:T(8,128)(2,1)S(1)}, bf16[16,8,128]{2,1,0:T(8,128)(2,1)S(1)}, u32[]{:S(2)}, u32[]{:S(2)}) collective-permute-start(bf16[16,8,128]{2,1,0:T(8,128)(2,1)S(1)} %get-tuple-element.13), channel_id=1, source_target_pairs={{32,64},{96,128},{160,192},{224,256},{288,320},{352,384},{416,448}... | collective-permute-start | bytes 98312 | tf_op jit(solution)/shard_map/ppermute | solution.py:141

commit v5 on v4

--- a/solution.py
+++ b/solution.py
@@ -13,7 +13,7 @@
 VMEM_LIMIT = 32 * 1024 * 1024
 
 
-FIRST_GATHER, FIRST_FRAMES = 8, 8
+FIRST_GATHER, FIRST_FRAMES = 10, 8
 
 
 def turned(order, first):
@@ -44,12 +44,13 @@
             yield pa, pb, total
 
 
-def conv_kernel(core_ref, weight_ref, latent_ref, bias_ref, own_ref, near_ref, far_ref, later_ref, earlier_ref):
+def conv_kernel(weight_ref, latent_ref, bias_ref, out_ref, wide_ref):
     channels = bias_ref.shape[0]
     rows = 16 * channels
+    after = channels - FIRST_FRAMES
     _, places = turned(latent_ref.shape[0], FIRST_GATHER)
     latent = in_turn(latent_ref, places)
-    for kt in (3, 0, 1, 2):
+    for kt, frame, kind in ((1, 0, 0), (2, 1, 0), (3, 0, 1), (0, 1, 1)):
         products = jnp.dot(
             weight_ref[kt * rows : (kt + 1) * rows, :], latent, preferred_element_type=jnp.float32
         )
@@ -59,27 +60,18 @@
             return products[start : start + channels, :]
 
         for pa, pb, total in spread(tap, channels):
-            if kt in (1, 2):
+            if kind == 0:
                 total = total + bias_ref[...]
             for half in (0, 1):
                 piece = total[:, half * 128 : (half + 1) * 128]
-                place = (pa * 2 + pb) * 2 + half
-                if kt == 3:
-                    later_ref[:, place, :] = piece
-                elif kt == 0:
-                    earlier_ref[:, place, :] = piece
-                else:
-                    own_ref[kt - 1, : channels - FIRST_FRAMES, place, :] = piece[FIRST_FRAMES:]
-                    own_ref[kt - 1, channels - FIRST_FRAMES :, place, :] = piece[:FIRST_FRAMES]
-    first = core_ref[0] == 0
-    later = jnp.concatenate([later_ref[FIRST_FRAMES:], later_ref[:FIRST_FRAMES]], 0)
-    earlier = jnp.concatenate([earlier_ref[FIRST_FRAMES:], earlier_ref[:FIRST_FRAMES]], 0)
-    near_ref[...] = jnp.where(first, later, earlier).astype(jnp.bfloat16)
-    far_ref[...] = jnp.where(first, earlier, later).astype(jnp.bfloat16)
+                place = kind * 8 + (pa * 2 + pb) * 2 + half
+                wide_ref[frame, :after, place, :] = piece[FIRST_FRAMES:]
+                wide_ref[frame, after:, place, :] = piece[:FIRST_FRAMES]
+    out_ref[...] = wide_ref[...].astype(jnp.bfloat16)
 
 
-def attend_kernel(piece_ref, query_ref, key_ref, out_ref, wide_ref, turned_ref):
-    wide_ref[...] = piece_ref[...].astype(jnp.float32)
+def attend_kernel(piece_ref, edge_ref, query_ref, key_ref, out_ref, wide_ref, turned_ref):
+    wide_ref[...] = piece_ref[:, :8, :].astype(jnp.float32) + edge_ref[...].astype(jnp.float32)
     channels = wide_ref.shape[0]
     column = channels // 2
     runs = [
@@ -94,8 +86,8 @@
         for source, target, size in runs:
             start = parity * channels + target
             turned_ref[start : start + size, columns] = wide_ref[source : source + size, place, :]
-    wide = turned_ref[...].T
-    tokens = wide.astype(jnp.bfloat16)
+    tokens = turned_ref[...].T.astype(jnp.bfloat16)
+    wide = tokens.astype(jnp.float32)
     queries = jnp.dot(tokens, query_ref[...], preferred_element_type=jnp.float32).astype(jnp.bfloat16)
     keys = jnp.dot(tokens, key_ref[...], preferred_element_type=jnp.float32).astype(jnp.bfloat16)
     scores = lax.dot_general(queries, keys, (((1,), (1,)), ((), ())), preferred_element_type=jnp.float32)
@@ -125,38 +117,46 @@
 
     rows, query_rows, key_rows = lax.optimization_barrier((rows, query_rows, key_rows))
 
-    edge = jax.ShapeDtypeStruct((channels, 8, 128), jnp.bfloat16)
-    own, near, far = pl.pallas_call(
+    vmem = pl.BlockSpec(memory_space=pltpu.VMEM)
+    params = pltpu.CompilerParams(vmem_limit_bytes=VMEM_LIMIT)
+    frames = pl.pallas_call(
         conv_kernel,
-        out_shape=(jax.ShapeDtypeStruct((2, channels, 8, 128), jnp.float32), edge, edge),
-        in_specs=[pl.BlockSpec(memory_space=pltpu.SMEM)] + [pl.BlockSpec(memory_space=pltpu.VMEM)] * 3,
-        out_specs=[pl.BlockSpec(memory_space=pltpu.VMEM)] * 3,
-        scratch_shapes=[pltpu.VMEM((channels, 8, 128), jnp.float32)] * 2,
-        compiler_params=pltpu.CompilerParams(vmem_limit_bytes=VMEM_LIMIT),
+        out_shape=jax.ShapeDtypeStruct((2, channels, 16, 128), jnp.bfloat16),
+        in_specs=[vmem] * 3,
+        out_specs=vmem,
+        scratch_shapes=[pltpu.VMEM((2, channels, 16, 128), jnp.float32)],
+        compiler_params=params,
         name="conv",
-    )(core.reshape(1), rows, gathered, conv_bias.reshape(channels, 1))
+    )(rows, gathered, conv_bias.reshape(channels, 1))
+    received = lax.all_to_all(
+        frames.reshape(2 * channels, 16, 128),
+        TILE,
+        split_axis=0,
+        concat_axis=0,
+        tiled=True,
+        axis_index_groups=[frames_order],
+    )
 
-    groups = lax.axis_size("pair") * lax.axis_size("core")
-    route = [(t, t + 1) for t in range(1, groups - 1, 2)] + [(t + 1, t) for t in range(1, groups - 1, 2)]
-    from_far = lax.ppermute(far, TM, route)
-    both = lax.all_gather(near, "core", axis=0)
-    from_near = jnp.where(core == 0, both[1], both[0])
-    to_first = jnp.where(core == 0, from_far, from_near).astype(jnp.float32)
-    to_second = jnp.where(core == 0, from_near, from_far).astype(jnp.float32)
-    frames = (own + jnp.stack([to_first, to_second])).astype(jnp.bfloat16)
-    received = lax.all_to_all(
-        frames.reshape(2 * channels, 8, 128), TILE, split_axis=0, concat_axis=0, tiled=True, axis_index_groups=[frames_order]
-    )
-    vmem = pl.BlockSpec(memory_space=pltpu.VMEM)
+    edge = received[:, 8:, :]
+    groups = lax.axis_size(TM)
+    column = lax.axis_index("xl")
+    forward = [(t * tiles + z, (t + 2) * tiles + z) for t in range(1, groups - 2, 2) for z in range(depth)]
+    backward = [(t * tiles + z, (t - 1) * tiles + z) for t in range(2, groups, 2) for z in range(depth, tiles)]
+    relayed = lax.ppermute(edge, TM + TILE, forward)
+    direct = lax.ppermute(edge, TM + TILE, backward)
+    shown = jnp.where((core == 1) & (column == 0), relayed, edge)
+    both = lax.all_gather(shown, "core", axis=0)
+    other = jnp.where(core == 0, both[1], both[0])
+    edge = jnp.where((core == 1) & (column == 1), direct, other)
     attended = pl.pallas_call(
         attend_kernel,
         out_shape=jax.ShapeDtypeStruct((CELLS, 4 * tiles), jnp.bfloat16),
-        in_specs=[vmem] * 3,
+        in_specs=[vmem] * 4,
         out_specs=vmem,
         scratch_shapes=[pltpu.VMEM((tiles, 8, 128), jnp.float32), pltpu.VMEM((4 * tiles, CELLS), jnp.float32)],
         compiler_params=pltpu.CompilerParams(vmem_limit_bytes=VMEM_LIMIT),
         name="attend",
-    )(received, query_rows, key_rows)
+    )(received, edge, query_rows, key_rows)
     return attended[None]
 
 

time: 59.9 us -> 59.5 us (level)
  starting transfers between devices: 21.6 us -> 18.4 us
  blocking collectives: 26.8 us -> 28.4 us
  waiting for transfers between devices: 4.24 us -> 4.9 us
    all_to_all x1, starting transfers between devices: 18.9 us -> 17.1 us  [local(): lax.all_to_all(copies, 'z', split_axis=0, concat_axis=0, tiled=True, axis...]
    all_to_all x1, waiting for transfers between devices: 3.17 us -> 4.89 us  [local(): lax.all_to_all(copies, 'z', split_axis=0, concat_axis=0, tiled=True, axis...]
    ppermute x1 -> x2, starting transfers between devices: 2.79 us -> 1.32 us  [the longest x1 0.66 us: local(): direct = lax.ppermute(edge, TM + TILE, backward)]
    all_to_all x1, blocking collectives: 17.4 us -> 18.8 us  [local(): lax.all_to_all(frames.reshape(2 * channels, 16, 128), TILE, split_axis=0,...]
    ppermute x1 -> x2, waiting for transfers between devices: 1.07 us -> 0.01 us  [the longest x1 0.01 us: local(): relayed = lax.ppermute(edge, TM + TILE, forward)]
  transfers between devices with their start and end apart: 2 -> 3, of which waited for: 2 -> 1; matrix products, arithmetic and copies ran while one was open for 4% -> 5% of each run, Pallas kernels for 0% -> 0%
where the time goes in v5:
time: 59.5 us; the launch traced here: 58.5 us
  blocking collectives  28.4 us (48%)
  starting transfers between devices  18.4 us (31%)
  waiting for transfers between devices  4.9 us (8%)
  local copies, waits for them, and re-layouts  4.68 us (8%)
  Pallas kernels  2.09 us (4%)
    all_to_all x1, blocking collectives, local(): lax.all_to_all(frames.reshape(2 * channels, 16, 128), TILE, split_axis=0,...  18.8 us
    all_to_all x1, starting transfers between devices, local(): lax.all_to_all(copies, 'z', split_axis=0, concat_axis=0, tiled=True, axis...  17.1 us
    all_gather x1, blocking collectives, local(): gathered = lax.all_gather(column, 'xl', axis=0, tiled=True)  5.63 us
    all_to_all x1, waiting for transfers between devices, local(): lax.all_to_all(copies, 'z', split_axis=0, concat_axis=0, tiled=True, axis...  4.89 us
    all_gather x1, blocking collectives, local(): both = lax.all_gather(shown, 'core', axis=0)  4.01 us
    transpose x1, local copies, waits for them, and re-layouts, local(): jnp.transpose(conv_weight, (1, 2, 3, 0, 4))  1.81 us
    pallas_call x1, Pallas kernels, local(): pl.pallas_call(attend_kernel, out_shape=jax.ShapeDtypeStruct((CELLS, 4 *...  1.46 us
    broadcast_in_dim x1, local copies, waits for them, and re-layouts, local(): copies = jnp.broadcast_to(latent, (depth,) + latent.shape[1:])  1.35 us
  transfers between devices with their start and end apart: 3, of which 1 were waited for; matrix products, arithmetic and copies ran while one was open for 5% of the time, Pallas kernels for 0%

profile of v5, /device:TPU:24, one launch (start us, length us, event | category | flops | bytes accessed | tf_op | source)
XLA Modules:
  0.0 58.5 jit_solution(16543660150299389190)
XLA Ops:
  0.0 1.3 %broadcast_in_dim.11 = bf16[16,16,256]{2,1,0:T(8,128)(2,1)} broadcast(bf16[16,256]{1,0:T(8,128)(2,1)} %bitcast.13), dimensions={1,2} | broadcast | bytes 139264 | tf_op jit(solution)/shard_map/broadcast_in_dim | solution.py:108
  1.3 17.1 %all-to-all-start = ((bf16[16,16,256]{2,1,0:T(8,128)(2,1)}), bf16[16,16,256]{2,1,0:T(8,128)(2,1)S(1)}, u32[]{:S(2)}, u32[]{:S(2)}) async-start(bf16[16,16,256]{2,1,0:T(8,128)(2,1)} %broadcast_in_dim.11), calls=%async_computation | async-start | bytes 262144 | tf_op jit(solution)/shard_map/all_to_all | solution.py:109
  18.4 1.8 %copy.8 = bf16[4,4,4,16,512]{4,3,2,1,0:T(8,128)(2,1)S(1)} copy(bf16[4,4,4,16,512]{4,2,1,0,3:T(4,128)(2,1)} %bitcast.12) | data formatting | bytes 2097152 | tf_op jit(solution)/shard_map/transpose | solution.py:113
  20.2 0.8 %dynamic-slice_bitcast_fusion = (bf16[128,128]{1,0:T(8,128)(2,1)S(1)}, bf16[128,128]{1,0:T(8,128)(2,1)S(1)}) fusion(bf16[16,128,128]{2,1,0:T(8,128)(2,1)} %param.9, s32[]{:T(128)S(6)} %select_n.36, bf16[16,128,128]{2,1,0:T(8,128)(2,1)} %param.8), kind=kLoop, calls=%fused_computation.3 | loop fusion | bytes 131076 | tf_op jit(solution)/shard_map/jit(dynamic_index_in_dim)/squeeze | solution.py:116
  21.0 0.0 copy-start
  21.0 0.7 %copy-done = f32[16]{0:T(128)S(1)} copy-done((f32[16]{0:T(128)S(1)}, f32[16]{0:T(128)}, u32[]{:S(2)}) %copy-start) | copy-done | bytes 88
  21.7 0.1 copy.9.bias_ref
  21.7 4.9 %all-to-all-done = bf16[16,16,256]{2,1,0:T(8,128)(2,1)S(1)} async-done(((bf16[16,16,256]{2,1,0:T(8,128)(2,1)}), bf16[16,16,256]{2,1,0:T(8,128)(2,1)S(1)}, u32[]{:S(2)}, u32[]{:S(2)}) %all-to-all-start) | async-done | bytes 131104 | tf_op jit(solution)/shard_map/all_to_all | solution.py:109
  26.6 5.6 %all_gather.9.latent_ref = bf16[32,16,256]{2,1,0:T(8,128)(2,1)S(1)} all-gather(bf16[16,16,256]{2,1,0:T(8,128)(2,1)S(1)} %all-to-all-done), channel_id=1, replica_groups=mesh['pair'=8,'core'=2,'xl'=2,'z'=16] {'xl'}, dimensions={0}, use_global_device_ids=true | all-gather | bytes 393216 | tf_op jit(solution)/shard_map/all_gather | solution.py:112
  32.3 0.6 %conv.1 = bf16[2,16,16,128]{3,2,1,0:T(8,128)(2,1)S(1)} custom-call(bf16[1024,512]{1,0:T(8,128)(2,1)S(1)} %bitcast.10, bf16[32,16,256]{2,1,0:T(8,128)(2,1)S(1)} %all_gather.9.latent_ref, f32[16,1]{1,0:T(8,128)S(1)} %copy.9.bias_ref), custom_call_target="tpu_custom_call" | custom-call | tf_op jit(solution)/shard_map/conv/pallas_call | solution.py:122
  32.9 18.8 %all_to_all.10.piece_ref = bf16[32,16,128]{2,1,0:T(8,128)(2,1)S(1)} all-to-all(bf16[32,16,128]{2,1,0:T(8,128)(2,1)S(1)} %bitcast.11), channel_id=1, replica_groups={{8,9,10,11,12,13,14,15,0,1,2,3,4,5,6,7,24,25,26,27,28,29,30,31,16,17,18..., dimensions={0} | all-to-all | bytes 262144 | tf_op jit(solution)/shard_map/all_to_all | solution.py:131
  51.7 0.7 %collective-permute-start.1 = (bf16[32,8,128]{2,1,0:T(8,128)(2,1)S(1)}, bf16[32,8,128]{2,1,0:T(8,128)(2,1)S(1)}, u32[]{:S(2)}, u32[]{:S(2)}) collective-permute-start(bf16[32,8,128]{2,1,0:T(8,128)(2,1)S(1)} %slice.14), channel_id=1, source_target_pairs={{32,96},{33,97},{34,98},{35,99},{36,100},{37,101},{38,102},{39,103... | collective-permute-start | bytes 196616 | tf_op jit(solution)/shard_map/ppermute | solution.py:145
  52.3 0.7 %collective-permute-start = (bf16[32,8,128]{2,1,0:T(8,128)(2,1)S(1)}, bf16[32,8,128]{2,1,0:T(8,128)(2,1)S(1)}, u32[]{:S(2)}, u32[]{:S(2)}) collective-permute-start(bf16[32,8,128]{2,1,0:T(8,128)(2,1)S(1)} %slice.14), channel_id=1, source_target_pairs={{80,48},{81,49},{82,50},{83,51},{84,52},{85,53},{86,54},{87,55},{8... | collective-permute-start | bytes 196616 | tf_op jit(solution)/shard_map/ppermute | solution.py:146
  53.0 0.0 collective-permute-done.1
  53.0 4.0 %all-gather = bf16[64,8,128]{2,1,0:T(8,128)(2,1)S(1)} all-gather(bf16[32,8,128]{2,1,0:T(8,128)(2,1)S(1)} %broadcast_select_fusion), channel_id=2, replica_groups=mesh['pair'=8,'core'=2,'xl'=2,'z'=16] {'core'}, dimensions={0}, use_global_device_ids=true | all-gather | bytes 196608 | tf_op jit(solution)/shard_map/all_gather | solution.py:148
  57.1 0.0 collective-permute-done
  57.1 1.5 %attend.1 = bf16[256,128]{1,0:T(8,128)(2,1)} custom-call(bf16[32,16,128]{2,1,0:T(8,128)(2,1)S(1)} %all_to_all.10.piece_ref, bf16[32,8,128]{2,1,0:T(8,128)(2,1)S(1)} %fusion.edge_ref, bf16[128,128]{1,0:T(8,128)(2,1)S(1)} %get-tuple-element.9.query_ref, bf16[128,128]{1,0:T(8,128)(2,1)S(1)} %get-tuple-element.10.key_ref), custom_call_target="tpu_custom_call" | custom-call | tf_op jit(solution)/shard_map/attend/pallas_call | solution.py:151
  (3 shorter events, 0.0 us)
Async XLA Ops:
  1.3 25.3 %all-to-all-start = ((bf16[16,16,256]{2,1,0:T(8,128)(2,1)}), bf16[16,16,256]{2,1,0:T(8,128)(2,1)S(1)}, u32[]{:S(2)}, u32[]{:S(2)}) async-start(bf16[16,16,256]{2,1,0:T(8,128)(2,1)} %broadcast_in_dim.11), calls=%async_computation | async-start | bytes 262144 | tf_op jit(solution)/shard_map/all_to_all | solution.py:109
  21.0 0.7 %copy-start = (f32[16]{0:T(128)S(1)}, f32[16]{0:T(128)}, u32[]{:S(2)}) copy-start(f32[16]{0:T(128)} %param.7) | copy-start | bytes 196
  51.7 1.4 %collective-permute-start.1 = (bf16[32,8,128]{2,1,0:T(8,128)(2,1)S(1)}, bf16[32,8,128]{2,1,0:T(8,128)(2,1)S(1)}, u32[]{:S(2)}, u32[]{:S(2)}) collective-permute-start(bf16[32,8,128]{2,1,0:T(8,128)(2,1)S(1)} %slice.14), channel_id=1, source_target_pairs={{32,96},{33,97},{34,98},{35,99},{36,100},{37,101},{38,102},{39,103... | collective-permute-start | bytes 196616 | tf_op jit(solution)/shard_map/ppermute | solution.py:145
  52.3 4.7 %collective-permute-start = (bf16[32,8,128]{2,1,0:T(8,128)(2,1)S(1)}, bf16[32,8,128]{2,1,0:T(8,128)(2,1)S(1)}, u32[]{:S(2)}, u32[]{:S(2)}) collective-permute-start(bf16[32,8,128]{2,1,0:T(8,128)(2,1)S(1)} %slice.14), channel_id=1, source_target_pairs={{80,48},{81,49},{82,50},{83,51},{84,52},{85,53},{86,54},{87,55},{8... | collective-permute-start | bytes 196616 | tf_op jit(solution)/shard_map/ppermute | solution.py:146

commit v6 on v5

--- a/solution.py
+++ b/solution.py
@@ -13,7 +13,7 @@
 VMEM_LIMIT = 32 * 1024 * 1024
 
 
-FIRST_GATHER, FIRST_FRAMES = 10, 8
+FIRST_GATHER, FIRST_FRAMES = 11, 8
 
 
 def turned(order, first):
@@ -86,16 +86,18 @@
         for source, target, size in runs:
             start = parity * channels + target
             turned_ref[start : start + size, columns] = wide_ref[source : source + size, place, :]
-    tokens = turned_ref[...].T.astype(jnp.bfloat16)
-    wide = tokens.astype(jnp.float32)
-    queries = jnp.dot(tokens, query_ref[...], preferred_element_type=jnp.float32).astype(jnp.bfloat16)
-    keys = jnp.dot(tokens, key_ref[...], preferred_element_type=jnp.float32).astype(jnp.bfloat16)
-    scores = lax.dot_general(queries, keys, (((1,), (1,)), ((), ())), preferred_element_type=jnp.float32)
+    across = turned_ref[...].astype(jnp.bfloat16)
+    wide = across.astype(jnp.float32).T
+    tokens = wide.astype(jnp.bfloat16)
+    contract_first = (((0,), (0,)), ((), ()))
+    queries = lax.dot_general(query_ref[...], across, contract_first, preferred_element_type=jnp.float32)
+    keys = jnp.dot(tokens, key_ref[...], preferred_element_type=jnp.float32)
+    scores = jnp.dot(keys.astype(jnp.bfloat16), queries.astype(jnp.bfloat16), preferred_element_type=jnp.float32)
     scores = scores * (tokens.shape[1] ** -0.5)
-    raised = jnp.exp(scores - jnp.max(scores, axis=1, keepdims=True))
-    weights = (raised / jnp.sum(raised, axis=1, keepdims=True)).astype(jnp.bfloat16)
-    mixed = jnp.dot(weights, tokens, preferred_element_type=jnp.float32)
-    out_ref[...] = (wide + mixed).astype(jnp.bfloat16)
+    raised = jnp.exp(scores - jnp.max(scores, axis=0, keepdims=True))
+    weights = (raised / jnp.sum(raised, axis=0, keepdims=True)).astype(jnp.bfloat16)
+    mixed = jnp.dot(across, weights, preferred_element_type=jnp.float32)
+    out_ref[...] = (wide + mixed.T).astype(jnp.bfloat16)
 
 
 def local(latent, conv_weight, conv_bias, query_weight, key_weight):

time: 59.5 us -> 59.4 us (level)
  starting transfers between devices: 18.4 us -> 17.5 us
  waiting for transfers between devices: 4.9 us -> 5.78 us
    all_to_all x1, starting transfers between devices: 17.1 us -> 16.2 us  [local(): lax.all_to_all(copies, 'z', split_axis=0, concat_axis=0, tiled=True, axis...]
    all_to_all x1, waiting for transfers between devices: 4.89 us -> 5.78 us  [local(): lax.all_to_all(copies, 'z', split_axis=0, concat_axis=0, tiled=True, axis...]
where the time goes in v6:
time: 59.4 us; the launch traced here: 58.5 us
  blocking collectives  28.4 us (48%)
  starting transfers between devices  17.5 us (29%)
  waiting for transfers between devices  5.78 us (10%)
  local copies, waits for them, and re-layouts  4.68 us (8%)
  Pallas kernels  2.02 us (3%)
    all_to_all x1, blocking collectives, local(): lax.all_to_all(frames.reshape(2 * channels, 16, 128), TILE, split_axis=0,...  18.8 us
    all_to_all x1, starting transfers between devices, local(): lax.all_to_all(copies, 'z', split_axis=0, concat_axis=0, tiled=True, axis...  16.2 us
    all_to_all x1, waiting for transfers between devices, local(): lax.all_to_all(copies, 'z', split_axis=0, concat_axis=0, tiled=True, axis...  5.78 us
    all_gather x1, blocking collectives, local(): gathered = lax.all_gather(column, 'xl', axis=0, tiled=True)  5.63 us
    all_gather x1, blocking collectives, local(): both = lax.all_gather(shown, 'core', axis=0)  4.02 us
    transpose x1, local copies, waits for them, and re-layouts, local(): jnp.transpose(conv_weight, (1, 2, 3, 0, 4))  1.81 us
    pallas_call x1, Pallas kernels, local(): pl.pallas_call(attend_kernel, out_shape=jax.ShapeDtypeStruct((CELLS, 4 *...  1.39 us
    broadcast_in_dim x1, local copies, waits for them, and re-layouts, local(): copies = jnp.broadcast_to(latent, (depth,) + latent.shape[1:])  1.35 us
  transfers between devices with their start and end apart: 3, of which 1 were waited for; matrix products, arithmetic and copies ran while one was open for 5% of the time, Pallas kernels for 0%

profile of v6, /device:TPU:24, one launch (start us, length us, event | category | flops | bytes accessed | tf_op | source)
XLA Modules:
  0.0 58.5 jit_solution(8825723402130387066)
XLA Ops:
  0.0 1.3 %broadcast_in_dim.11 = bf16[16,16,256]{2,1,0:T(8,128)(2,1)} broadcast(bf16[16,256]{1,0:T(8,128)(2,1)} %bitcast.13), dimensions={1,2} | broadcast | bytes 139264 | tf_op jit(solution)/shard_map/broadcast_in_dim | solution.py:110
  1.3 16.2 %all-to-all-start = ((bf16[16,16,256]{2,1,0:T(8,128)(2,1)}), bf16[16,16,256]{2,1,0:T(8,128)(2,1)S(1)}, u32[]{:S(2)}, u32[]{:S(2)}) async-start(bf16[16,16,256]{2,1,0:T(8,128)(2,1)} %broadcast_in_dim.11), calls=%async_computation | async-start | bytes 262144 | tf_op jit(solution)/shard_map/all_to_all | solution.py:111
  17.5 1.8 %copy.8 = bf16[4,4,4,16,512]{4,3,2,1,0:T(8,128)(2,1)S(1)} copy(bf16[4,4,4,16,512]{4,2,1,0,3:T(4,128)(2,1)} %bitcast.12) | data formatting | bytes 2097152 | tf_op jit(solution)/shard_map/transpose | solution.py:115
  19.3 0.8 %dynamic-slice_bitcast_fusion = (bf16[128,128]{1,0:T(8,128)(2,1)S(1)}, bf16[128,128]{1,0:T(8,128)(2,1)S(1)}) fusion(bf16[16,128,128]{2,1,0:T(8,128)(2,1)} %param.9, s32[]{:T(128)S(6)} %select_n.36, bf16[16,128,128]{2,1,0:T(8,128)(2,1)} %param.8), kind=kLoop, calls=%fused_computation.3 | loop fusion | bytes 131076 | tf_op jit(solution)/shard_map/jit(dynamic_index_in_dim)/squeeze | solution.py:118
  20.1 0.0 copy-start
  20.1 0.7 %copy-done = f32[16]{0:T(128)S(1)} copy-done((f32[16]{0:T(128)S(1)}, f32[16]{0:T(128)}, u32[]{:S(2)}) %copy-start) | copy-done | bytes 88
  20.8 0.1 copy.9.bias_ref
  20.8 5.8 %all-to-all-done = bf16[16,16,256]{2,1,0:T(8,128)(2,1)S(1)} async-done(((bf16[16,16,256]{2,1,0:T(8,128)(2,1)}), bf16[16,16,256]{2,1,0:T(8,128)(2,1)S(1)}, u32[]{:S(2)}, u32[]{:S(2)}) %all-to-all-start) | async-done | bytes 131104 | tf_op jit(solution)/shard_map/all_to_all | solution.py:111
  26.6 5.6 %all_gather.9.latent_ref = bf16[32,16,256]{2,1,0:T(8,128)(2,1)S(1)} all-gather(bf16[16,16,256]{2,1,0:T(8,128)(2,1)S(1)} %all-to-all-done), channel_id=1, replica_groups=mesh['pair'=8,'core'=2,'xl'=2,'z'=16] {'xl'}, dimensions={0}, use_global_device_ids=true | all-gather | bytes 393216 | tf_op jit(solution)/shard_map/all_gather | solution.py:114
  32.3 0.6 %conv.1 = bf16[2,16,16,128]{3,2,1,0:T(8,128)(2,1)S(1)} custom-call(bf16[1024,512]{1,0:T(8,128)(2,1)S(1)} %bitcast.10, bf16[32,16,256]{2,1,0:T(8,128)(2,1)S(1)} %all_gather.9.latent_ref, f32[16,1]{1,0:T(8,128)S(1)} %copy.9.bias_ref), custom_call_target="tpu_custom_call" | custom-call | tf_op jit(solution)/shard_map/conv/pallas_call | solution.py:124
  32.9 18.8 %all_to_all.10.piece_ref = bf16[32,16,128]{2,1,0:T(8,128)(2,1)S(1)} all-to-all(bf16[32,16,128]{2,1,0:T(8,128)(2,1)S(1)} %bitcast.11), channel_id=1, replica_groups={{8,9,10,11,12,13,14,15,0,1,2,3,4,5,6,7,24,25,26,27,28,29,30,31,16,17,18..., dimensions={0} | all-to-all | bytes 262144 | tf_op jit(solution)/shard_map/all_to_all | solution.py:133
  51.7 0.7 %collective-permute-start.1 = (bf16[32,8,128]{2,1,0:T(8,128)(2,1)S(1)}, bf16[32,8,128]{2,1,0:T(8,128)(2,1)S(1)}, u32[]{:S(2)}, u32[]{:S(2)}) collective-permute-start(bf16[32,8,128]{2,1,0:T(8,128)(2,1)S(1)} %slice.14), channel_id=1, source_target_pairs={{32,96},{33,97},{34,98},{35,99},{36,100},{37,101},{38,102},{39,103... | collective-permute-start | bytes 196616 | tf_op jit(solution)/shard_map/ppermute | solution.py:147
  52.4 0.7 %collective-permute-start = (bf16[32,8,128]{2,1,0:T(8,128)(2,1)S(1)}, bf16[32,8,128]{2,1,0:T(8,128)(2,1)S(1)}, u32[]{:S(2)}, u32[]{:S(2)}) collective-permute-start(bf16[32,8,128]{2,1,0:T(8,128)(2,1)S(1)} %slice.14), channel_id=1, source_target_pairs={{80,48},{81,49},{82,50},{83,51},{84,52},{85,53},{86,54},{87,55},{8... | collective-permute-start | bytes 196616 | tf_op jit(solution)/shard_map/ppermute | solution.py:148
  53.0 0.0 collective-permute-done.1
  53.1 4.0 %all-gather = bf16[64,8,128]{2,1,0:T(8,128)(2,1)S(1)} all-gather(bf16[32,8,128]{2,1,0:T(8,128)(2,1)S(1)} %broadcast_select_fusion), channel_id=2, replica_groups=mesh['pair'=8,'core'=2,'xl'=2,'z'=16] {'core'}, dimensions={0}, use_global_device_ids=true | all-gather | bytes 196608 | tf_op jit(solution)/shard_map/all_gather | solution.py:150
  57.1 0.0 collective-permute-done
  57.1 1.4 %attend.1 = bf16[256,128]{1,0:T(8,128)(2,1)} custom-call(bf16[32,16,128]{2,1,0:T(8,128)(2,1)S(1)} %all_to_all.10.piece_ref, bf16[32,8,128]{2,1,0:T(8,128)(2,1)S(1)} %fusion.edge_ref, bf16[128,128]{1,0:T(8,128)(2,1)S(1)} %get-tuple-element.9.query_ref, bf16[128,128]{1,0:T(8,128)(2,1)S(1)} %get-tuple-element.10.key_ref), custom_call_target="tpu_custom_call" | custom-call | tf_op jit(solution)/shard_map/attend/pallas_call | solution.py:153
  (3 shorter events, 0.0 us)
Async XLA Ops:
  1.3 25.3 %all-to-all-start = ((bf16[16,16,256]{2,1,0:T(8,128)(2,1)}), bf16[16,16,256]{2,1,0:T(8,128)(2,1)S(1)}, u32[]{:S(2)}, u32[]{:S(2)}) async-start(bf16[16,16,256]{2,1,0:T(8,128)(2,1)} %broadcast_in_dim.11), calls=%async_computation | async-start | bytes 262144 | tf_op jit(solution)/shard_map/all_to_all | solution.py:111
  20.1 0.7 %copy-start = (f32[16]{0:T(128)S(1)}, f32[16]{0:T(128)}, u32[]{:S(2)}) copy-start(f32[16]{0:T(128)} %param.7) | copy-start | bytes 196
  51.7 1.4 %collective-permute-start.1 = (bf16[32,8,128]{2,1,0:T(8,128)(2,1)S(1)}, bf16[32,8,128]{2,1,0:T(8,128)(2,1)S(1)}, u32[]{:S(2)}, u32[]{:S(2)}) collective-permute-start(bf16[32,8,128]{2,1,0:T(8,128)(2,1)S(1)} %slice.14), channel_id=1, source_target_pairs={{32,96},{33,97},{34,98},{35,99},{36,100},{37,101},{38,102},{39,103... | collective-permute-start | bytes 196616 | tf_op jit(solution)/shard_map/ppermute | solution.py:147
  52.4 4.7 %collective-permute-start = (bf16[32,8,128]{2,1,0:T(8,128)(2,1)S(1)}, bf16[32,8,128]{2,1,0:T(8,128)(2,1)S(1)}, u32[]{:S(2)}, u32[]{:S(2)}) collective-permute-start(bf16[32,8,128]{2,1,0:T(8,128)(2,1)S(1)} %slice.14), channel_id=1, source_target_pairs={{80,48},{81,49},{82,50},{83,51},{84,52},{85,53},{86,54},{87,55},{8... | collective-permute-start | bytes 196616 | tf_op jit(solution)/shard_map/ppermute | solution.py:148

commit v7 on v4

--- a/solution.py
+++ b/solution.py
@@ -13,7 +13,7 @@
 VMEM_LIMIT = 32 * 1024 * 1024
 
 
-FIRST_GATHER, FIRST_FRAMES = 8, 8
+FIRST_GATHER, FIRST_FRAMES = 11, 8
 
 
 def turned(order, first):
@@ -44,7 +44,7 @@
             yield pa, pb, total
 
 
-def conv_kernel(core_ref, weight_ref, latent_ref, bias_ref, own_ref, near_ref, far_ref, later_ref, earlier_ref):
+def conv_kernel(weight_ref, latent_ref, bias_ref, own_ref, next_ref, last_ref, later_ref, earlier_ref):
     channels = bias_ref.shape[0]
     rows = 16 * channels
     _, places = turned(latent_ref.shape[0], FIRST_GATHER)
@@ -71,11 +71,14 @@
                 else:
                     own_ref[kt - 1, : channels - FIRST_FRAMES, place, :] = piece[FIRST_FRAMES:]
                     own_ref[kt - 1, channels - FIRST_FRAMES :, place, :] = piece[:FIRST_FRAMES]
-    first = core_ref[0] == 0
     later = jnp.concatenate([later_ref[FIRST_FRAMES:], later_ref[:FIRST_FRAMES]], 0)
     earlier = jnp.concatenate([earlier_ref[FIRST_FRAMES:], earlier_ref[:FIRST_FRAMES]], 0)
-    near_ref[...] = jnp.where(first, later, earlier).astype(jnp.bfloat16)
-    far_ref[...] = jnp.where(first, earlier, later).astype(jnp.bfloat16)
+    next_ref[...] = later
+    last_ref[...] = earlier.astype(jnp.bfloat16)
+
+
+def leave_kernel(own_ref, next_ref, last_ref):
+    pass
 
 
 def attend_kernel(piece_ref, query_ref, key_ref, out_ref, wide_ref, turned_ref):
@@ -94,16 +97,18 @@
         for source, target, size in runs:
             start = parity * channels + target
             turned_ref[start : start + size, columns] = wide_ref[source : source + size, place, :]
-    wide = turned_ref[...].T
-    tokens = wide.astype(jnp.bfloat16)
-    queries = jnp.dot(tokens, query_ref[...], preferred_element_type=jnp.float32).astype(jnp.bfloat16)
-    keys = jnp.dot(tokens, key_ref[...], preferred_element_type=jnp.float32).astype(jnp.bfloat16)
-    scores = lax.dot_general(queries, keys, (((1,), (1,)), ((), ())), preferred_element_type=jnp.float32)
+    across = turned_ref[...]
+    wide = across.T
+    tokens, across = wide.astype(jnp.bfloat16), across.astype(jnp.bfloat16)
+    contract_first = (((0,), (0,)), ((), ()))
+    queries = lax.dot_general(query_ref[...], across, contract_first, preferred_element_type=jnp.float32)
+    keys = jnp.dot(tokens, key_ref[...], preferred_element_type=jnp.float32)
+    scores = jnp.dot(keys.astype(jnp.bfloat16), queries.astype(jnp.bfloat16), preferred_element_type=jnp.float32)
     scores = scores * (tokens.shape[1] ** -0.5)
-    raised = jnp.exp(scores - jnp.max(scores, axis=1, keepdims=True))
-    weights = (raised / jnp.sum(raised, axis=1, keepdims=True)).astype(jnp.bfloat16)
-    mixed = jnp.dot(weights, tokens, preferred_element_type=jnp.float32)
-    out_ref[...] = (wide + mixed).astype(jnp.bfloat16)
+    raised = jnp.exp(scores - jnp.max(scores, axis=0, keepdims=True))
+    weights = (raised / jnp.sum(raised, axis=0, keepdims=True)).astype(jnp.bfloat16)
+    mixed = jnp.dot(across, weights, preferred_element_type=jnp.float32)
+    out_ref[...] = (wide + mixed.T).astype(jnp.bfloat16)
 
 
 def local(latent, conv_weight, conv_bias, query_weight, key_weight):
@@ -117,7 +122,6 @@
     column = lax.all_to_all(
         copies, "z", split_axis=0, concat_axis=0, tiled=True, axis_index_groups=[gather_order[:depth]]
     )
-    gathered = lax.all_gather(column, "xl", axis=0, tiled=True)
     rows = jnp.transpose(conv_weight, (1, 2, 3, 0, 4)).reshape(-1, conv_weight.shape[-1])
     head = lax.axis_index(TILE) % HEADS
     query_rows = lax.dynamic_index_in_dim(query_weight, head, 0, keepdims=False)
@@ -125,24 +129,47 @@
 
     rows, query_rows, key_rows = lax.optimization_barrier((rows, query_rows, key_rows))
 
+    vmem = pl.BlockSpec(memory_space=pltpu.VMEM)
     edge = jax.ShapeDtypeStruct((channels, 8, 128), jnp.bfloat16)
-    own, near, far = pl.pallas_call(
-        conv_kernel,
-        out_shape=(jax.ShapeDtypeStruct((2, channels, 8, 128), jnp.float32), edge, edge),
-        in_specs=[pl.BlockSpec(memory_space=pltpu.SMEM)] + [pl.BlockSpec(memory_space=pltpu.VMEM)] * 3,
-        out_specs=[pl.BlockSpec(memory_space=pltpu.VMEM)] * 3,
-        scratch_shapes=[pltpu.VMEM((channels, 8, 128), jnp.float32)] * 2,
-        compiler_params=pltpu.CompilerParams(vmem_limit_bytes=VMEM_LIMIT),
-        name="conv",
-    )(core.reshape(1), rows, gathered, conv_bias.reshape(channels, 1))
+    shapes = (
+        jax.ShapeDtypeStruct((2, channels, 8, 128), jnp.float32),
+        jax.ShapeDtypeStruct(edge.shape, jnp.float32),
+        edge,
+    )
+    biases = conv_bias.reshape(channels, 1)
 
+    def work(column, rows, biases):
+        gathered = lax.all_gather(column, "xl", axis=0, tiled=True)
+        return tuple(
+            pl.pallas_call(
+                conv_kernel,
+                out_shape=shapes,
+                in_specs=[vmem] * 3,
+                out_specs=[vmem] * 3,
+                scratch_shapes=[pltpu.VMEM((channels, 8, 128), jnp.float32)] * 2,
+                compiler_params=pltpu.CompilerParams(vmem_limit_bytes=VMEM_LIMIT),
+                name="conv",
+            )(rows, gathered, biases)
+        )
+
+    def leave(column, rows, biases):
+        return tuple(
+            pl.pallas_call(
+                leave_kernel, out_shape=shapes, out_specs=[pl.BlockSpec(memory_space=pl.ANY)] * 3, name="leave"
+            )()
+        )
+
+    ones = lax.cond(core == 1, work, leave, column, rows, biases)
     groups = lax.axis_size("pair") * lax.axis_size("core")
-    route = [(t, t + 1) for t in range(1, groups - 1, 2)] + [(t + 1, t) for t in range(1, groups - 1, 2)]
-    from_far = lax.ppermute(far, TM, route)
-    both = lax.all_gather(near, "core", axis=0)
-    from_near = jnp.where(core == 0, both[1], both[0])
-    to_first = jnp.where(core == 0, from_far, from_near).astype(jnp.float32)
-    to_second = jnp.where(core == 0, from_near, from_far).astype(jnp.float32)
+    from_last = lax.ppermute(ones[1], TM, [(t, t + 1) for t in range(1, groups - 1, 2)])
+    column, ones = lax.optimization_barrier((column, ones))
+    zeros = lax.cond(core == 0, work, leave, column, rows, biases)
+    own = jnp.where(core == 0, zeros[0], ones[0])
+    to_next, to_last = zeros[1], jnp.where(core == 0, zeros[2], ones[2])
+    from_next = lax.ppermute(zeros[2], TM, [(t, t - 1) for t in range(2, groups, 2)])
+    both = lax.all_gather(jnp.where(core == 0, to_next.astype(jnp.bfloat16), to_last), "core", axis=0)
+    to_first = jnp.where(core == 0, from_last, both[0].astype(jnp.float32))
+    to_second = jnp.where(core == 0, both[1], from_next).astype(jnp.float32)
     frames = (own + jnp.stack([to_first, to_second])).astype(jnp.bfloat16)
     received = lax.all_to_all(
         frames.reshape(2 * channels, 8, 128), TILE, split_axis=0, concat_axis=0, tiled=True, axis_index_groups=[frames_order]

time: 59.9 us -> 58.6 us (0.978); the launches traced: 59.5 us -> 57.6 us
  waiting for transfers between devices: 4.24 us -> 6.52 us
  starting transfers between devices: 21.6 us -> 19.7 us
  blocking collectives: 26.8 us -> 25.2 us
  local copies, waits for them, and re-layouts: 4.68 us -> 4.03 us
    all_to_all x1, waiting for transfers between devices: 3.17 us -> 6.52 us  [local(): lax.all_to_all(copies, 'z', split_axis=0, concat_axis=0, tiled=True, axis...]
    all_to_all x1, starting transfers between devices: 18.9 us -> 16.2 us  [local(): lax.all_to_all(copies, 'z', split_axis=0, concat_axis=0, tiled=True, axis...]
    all_gather x2, blocking collectives: 9.39 us -> 7.49 us  [the longest x1 5.63 us: work(): gathered = lax.all_gather(column, 'xl', axis=0, tiled=True)]
    ppermute x1 -> x2, waiting for transfers between devices: 1.07 us -> 0.01 us  [the longest x1 0.01 us: local(): lax.ppermute(ones[1], TM, [(t, t + 1) for t in range(1, groups - 1, 2)])]
    ppermute x1 -> x2, starting transfers between devices: 2.79 us -> 3.58 us  [the longest x1 2.3 us: local(): lax.ppermute(zeros[2], TM, [(t, t - 1) for t in range(2, groups, 2)])]
    unnamed x2, local copies, waits for them, and re-layouts: 0.65 us -> 0.01 us
  transfers between devices with their start and end apart: 2 -> 3, of which waited for: 2 -> 1; matrix products, arithmetic and copies ran while one was open for 4% -> 5% of each run, Pallas kernels for 0% -> 1%
where the time goes in v7:
time: 58.6 us; the launch traced here: 57.6 us
  blocking collectives  25.2 us (43%)
  starting transfers between devices  19.7 us (34%)
  waiting for transfers between devices  6.52 us (11%)
  local copies, waits for them, and re-layouts  4.03 us (7%)
  Pallas kernels  2.01 us (3%)
    all_to_all x1, blocking collectives, local(): lax.all_to_all(frames.reshape(2 * channels, 8, 128), TILE, split_axis=0,...  17.7 us
    all_to_all x1, starting transfers between devices, local(): lax.all_to_all(copies, 'z', split_axis=0, concat_axis=0, tiled=True, axis...  16.2 us
    all_to_all x1, waiting for transfers between devices, local(): lax.all_to_all(copies, 'z', split_axis=0, concat_axis=0, tiled=True, axis...  6.52 us
    all_gather x1, blocking collectives, work(): gathered = lax.all_gather(column, 'xl', axis=0, tiled=True)  5.63 us
    ppermute x1, starting transfers between devices, local(): lax.ppermute(zeros[2], TM, [(t, t - 1) for t in range(2, groups, 2)])  2.3 us
    all_gather x1, blocking collectives, local(): lax.all_gather(jnp.where(core == 0, to_next.astype(jnp.bfloat16), to_last...  1.85 us
    transpose x1, local copies, waits for them, and re-layouts, local(): jnp.transpose(conv_weight, (1, 2, 3, 0, 4))  1.81 us
    pallas_call x1, Pallas kernels, local(): pl.pallas_call(attend_kernel, out_shape=jax.ShapeDtypeStruct((CELLS, 4 *...  1.38 us
  transfers between devices with their start and end apart: 3, of which 1 were waited for; matrix products, arithmetic and copies ran while one was open for 5% of the time, Pallas kernels for 1%

profile of v7, /device:TPU:24, one launch (start us, length us, event | category | flops | bytes accessed | tf_op | source)
XLA Modules:
  0.0 57.6 jit_solution(12312592322392413368)
XLA Ops:
  0.0 1.4 %broadcast_in_dim.11 = bf16[16,16,256]{2,1,0:T(8,128)(2,1)} broadcast(bf16[16,256]{1,0:T(8,128)(2,1)} %bitcast.21), dimensions={1,2} | broadcast | bytes 139264 | tf_op jit(solution)/shard_map/broadcast_in_dim | solution.py:121
  1.4 16.2 %all-to-all-start = ((bf16[16,16,256]{2,1,0:T(8,128)(2,1)}), bf16[16,16,256]{2,1,0:T(8,128)(2,1)S(1)}, u32[]{:S(2)}, u32[]{:S(2)}) async-start(bf16[16,16,256]{2,1,0:T(8,128)(2,1)} %broadcast_in_dim.11), calls=%async_computation | async-start | bytes 262144 | tf_op jit(solution)/shard_map/all_to_all | solution.py:122
  17.5 1.8 %copy.9 = bf16[4,4,4,16,512]{4,3,2,1,0:T(8,128)(2,1)S(1)} copy(bf16[4,4,4,16,512]{4,2,1,0,3:T(4,128)(2,1)} %bitcast.19) | data formatting | bytes 2097152 | tf_op jit(solution)/shard_map/transpose | solution.py:125
  19.3 0.8 %dynamic-slice_bitcast_fusion = (bf16[128,128]{1,0:T(8,128)(2,1)S(1)}, bf16[128,128]{1,0:T(8,128)(2,1)S(1)}) fusion(bf16[16,128,128]{2,1,0:T(8,128)(2,1)} %param.13, s32[]{:T(128)S(6)} %select_n.44, bf16[16,128,128]{2,1,0:T(8,128)(2,1)} %param.12), kind=kLoop, calls=%fused_computation.8 | loop fusion | bytes 131076 | tf_op jit(solution)/shard_map/jit(dynamic_index_in_dim)/squeeze | solution.py:128
  20.1 0.0 copy-start
  20.1 6.5 %all-to-all-done = bf16[16,16,256]{2,1,0:T(8,128)(2,1)S(1)} async-done(((bf16[16,16,256]{2,1,0:T(8,128)(2,1)}), bf16[16,16,256]{2,1,0:T(8,128)(2,1)S(1)}, u32[]{:S(2)}, u32[]{:S(2)}) %all-to-all-start) | async-done | bytes 131104 | tf_op jit(solution)/shard_map/all_to_all | solution.py:122
  26.6 0.0 copy-done
  26.6 1.3 %collective-permute-start = (f32[16,8,128]{2,1,0:T(8,128)S(1)}, f32[16,8,128]{2,1,0:T(8,128)S(1)}, u32[]{:S(2)}, u32[]{:S(2)}) collective-permute-start(f32[16,8,128]{2,1,0:T(8,128)S(1)} %get-tuple-element.54), channel_id=1, source_target_pairs={{32,64},{96,128},{160,192},{224,256},{288,320},{352,384},{416,448}... | collective-permute-start | bytes 196616 | tf_op jit(solution)/shard_map/ppermute | solution.py:164
  27.9 6.4 %conditional.4 = (f32[2,16,8,128]{3,2,1,0:T(8,128)S(1)}, bf16[16,8,128]{2,1,0:T(8,128)(2,1)S(1)}, f32[16,8,128]{2,1,0:T(8,128)S(1)}) conditional(s32[]{:T(128)} %convert_element_type.22, () %tuple.26, (bf16[16,16,256]{2,1,0:T(8,128)(2,1)S(1)}, bf16[1024,512]{1,0:T(8,128)(2,1)S(1)}, f32[16,1]{0,1:T(1,128)S(1)}) %tuple.46), branch_computations={%region_2.3_spmd, %region_3.4_spmd} | conditional | bytes 393368
  27.9 0.1 copy.11.bias_ref
  28.0 5.6 %all_gather.9.latent_ref = bf16[32,16,256]{2,1,0:T(8,128)(2,1)S(1)} all-gather(bf16[16,16,256]{2,1,0:T(8,128)(2,1)S(1)} %get-tuple-element.35), channel_id=1, replica_groups=mesh['pair'=8,'core'=2,'xl'=2,'z'=16] {'xl'}, dimensions={0}, use_global_device_ids=true | all-gather | bytes 393216 | tf_op jit(solution)/shard_map/cond/branch_1_fun/all_gather | solution.py:142
  33.7 0.6 %conv.3 = (f32[2,16,8,128]{3,2,1,0:T(8,128)S(1)}, f32[16,8,128]{2,1,0:T(8,128)S(1)}, bf16[16,8,128]{2,1,0:T(8,128)(2,1)S(1)}) custom-call(bf16[1024,512]{1,0:T(8,128)(2,1)S(1)} %get-tuple-element.34.weight_ref, bf16[32,16,256]{2,1,0:T(8,128)(2,1)S(1)} %all_gather.9.latent_ref, f32[16,1]{1,0:T(8,128)S(1)} %copy.11.bias_ref), custom_call_target="tpu_custom_call" | custom-call | tf_op jit(solution)/shard_map/cond/branch_1_fun/conv/pallas_call | solution.py:144
  34.3 2.3 %collective-permute-start.1 = (bf16[16,8,128]{2,1,0:T(8,128)(2,1)S(1)}, bf16[16,8,128]{2,1,0:T(8,128)(2,1)S(1)}, u32[]{:S(2)}, u32[]{:S(2)}) collective-permute-start(bf16[16,8,128]{2,1,0:T(8,128)(2,1)S(1)} %get-tuple-element.60), channel_id=1, source_target_pairs={{64,32},{128,96},{192,160},{256,224},{320,288},{384,352},{448,416}... | collective-permute-start | bytes 98312 | tf_op jit(solution)/shard_map/ppermute | solution.py:169
  36.6 1.9 %all-gather = bf16[32,8,128]{2,1,0:T(8,128)(2,1)S(1)} all-gather(bf16[16,8,128]{2,1,0:T(8,128)(2,1)S(1)} %select_select_fusion), channel_id=2, replica_groups=mesh['pair'=8,'core'=2,'xl'=2,'z'=16] {'core'}, dimensions={0}, use_global_device_ids=true | all-gather | bytes 98304 | tf_op jit(solution)/shard_map/all_gather | solution.py:170
  38.5 0.0 collective-permute-done.1
  38.5 0.0 collective-permute-done
  38.6 17.7 %all_to_all.10.piece_ref = bf16[32,8,128]{2,1,0:T(8,128)(2,1)S(1)} all-to-all(bf16[32,8,128]{2,1,0:T(8,128)(2,1)S(1)} %bitcast.20), channel_id=1, replica_groups={{8,9,10,11,12,13,14,15,0,1,2,3,4,5,6,7,24,25,26,27,28,29,30,31,16,17,18..., dimensions={0} | all-to-all | bytes 131072 | tf_op jit(solution)/shard_map/all_to_all | solution.py:174
  56.2 1.4 %attend.1 = bf16[256,128]{1,0:T(8,128)(2,1)} custom-call(bf16[32,8,128]{2,1,0:T(8,128)(2,1)S(1)} %all_to_all.10.piece_ref, bf16[128,128]{1,0:T(8,128)(2,1)S(1)} %get-tuple-element.62.query_ref, bf16[128,128]{1,0:T(8,128)(2,1)S(1)} %get-tuple-element.63.key_ref), custom_call_target="tpu_custom_call" | custom-call | tf_op jit(solution)/shard_map/attend/pallas_call | solution.py:178
  (6 shorter events, 0.1 us)
Async XLA Ops:
  1.4 25.3 %all-to-all-start = ((bf16[16,16,256]{2,1,0:T(8,128)(2,1)}), bf16[16,16,256]{2,1,0:T(8,128)(2,1)S(1)}, u32[]{:S(2)}, u32[]{:S(2)}) async-start(bf16[16,16,256]{2,1,0:T(8,128)(2,1)} %broadcast_in_dim.11), calls=%async_computation | async-start | bytes 262144 | tf_op jit(solution)/shard_map/all_to_all | solution.py:122
  20.1 6.5 %copy-start = (f32[16]{0:T(128)S(1)}, f32[16]{0:T(128)}, u32[]{:S(2)}) copy-start(f32[16]{0:T(128)} %param.11) | copy-start | bytes 196
  26.6 11.9 %collective-permute-start = (f32[16,8,128]{2,1,0:T(8,128)S(1)}, f32[16,8,128]{2,1,0:T(8,128)S(1)}, u32[]{:S(2)}, u32[]{:S(2)}) collective-permute-start(f32[16,8,128]{2,1,0:T(8,128)S(1)} %get-tuple-element.54), channel_id=1, source_target_pairs={{32,64},{96,128},{160,192},{224,256},{288,320},{352,384},{416,448}... | collective-permute-start | bytes 196616 | tf_op jit(solution)/shard_map/ppermute | solution.py:164
  34.3 4.2 %collective-permute-start.1 = (bf16[16,8,128]{2,1,0:T(8,128)(2,1)S(1)}, bf16[16,8,128]{2,1,0:T(8,128)(2,1)S(1)}, u32[]{:S(2)}, u32[]{:S(2)}) collective-permute-start(bf16[16,8,128]{2,1,0:T(8,128)(2,1)S(1)} %get-tuple-element.60), channel_id=1, source_target_pairs={{64,32},{128,96},{192,160},{256,224},{320,288},{384,352},{448,416}... | collective-permute-start | bytes 98312 | tf_op jit(solution)/shard_map/ppermute | solution.py:169

commit v8 on v7

--- a/solution.py
+++ b/solution.py
@@ -73,7 +73,7 @@
                     own_ref[kt - 1, channels - FIRST_FRAMES :, place, :] = piece[:FIRST_FRAMES]
     later = jnp.concatenate([later_ref[FIRST_FRAMES:], later_ref[:FIRST_FRAMES]], 0)
     earlier = jnp.concatenate([earlier_ref[FIRST_FRAMES:], earlier_ref[:FIRST_FRAMES]], 0)
-    next_ref[...] = later
+    next_ref[...] = later.astype(jnp.bfloat16)
     last_ref[...] = earlier.astype(jnp.bfloat16)
 
 
@@ -131,11 +131,7 @@
 
     vmem = pl.BlockSpec(memory_space=pltpu.VMEM)
     edge = jax.ShapeDtypeStruct((channels, 8, 128), jnp.bfloat16)
-    shapes = (
-        jax.ShapeDtypeStruct((2, channels, 8, 128), jnp.float32),
-        jax.ShapeDtypeStruct(edge.shape, jnp.float32),
-        edge,
-    )
+    shapes = (jax.ShapeDtypeStruct((2, channels, 8, 128), jnp.float32), edge, edge)
     biases = conv_bias.reshape(channels, 1)
 
     def work(column, rows, biases):
@@ -167,8 +163,8 @@
     own = jnp.where(core == 0, zeros[0], ones[0])
     to_next, to_last = zeros[1], jnp.where(core == 0, zeros[2], ones[2])
     from_next = lax.ppermute(zeros[2], TM, [(t, t - 1) for t in range(2, groups, 2)])
-    both = lax.all_gather(jnp.where(core == 0, to_next.astype(jnp.bfloat16), to_last), "core", axis=0)
-    to_first = jnp.where(core == 0, from_last, both[0].astype(jnp.float32))
+    both = lax.all_gather(jnp.where(core == 0, to_next, to_last), "core", axis=0)
+    to_first = jnp.where(core == 0, from_last, both[0]).astype(jnp.float32)
     to_second = jnp.where(core == 0, both[1], from_next).astype(jnp.float32)
     frames = (own + jnp.stack([to_first, to_second])).astype(jnp.bfloat16)
     received = lax.all_to_all(

time: 58.6 us -> 58.5 us (level)
  no operation moved by 1% of the time
where the time goes in v8:
time: 58.5 us; the launch traced here: 57.5 us
  blocking collectives  25.1 us (43%)
  starting transfers between devices  19.7 us (34%)
  waiting for transfers between devices  6.52 us (11%)
  local copies, waits for them, and re-layouts  4.03 us (7%)
  Pallas kernels  2.01 us (3%)
    all_to_all x1, blocking collectives, local(): lax.all_to_all(frames.reshape(2 * channels, 8, 128), TILE, split_axis=0,...  17.6 us
    all_to_all x1, starting transfers between devices, local(): lax.all_to_all(copies, 'z', split_axis=0, concat_axis=0, tiled=True, axis...  16.2 us
    all_to_all x1, waiting for transfers between devices, local(): lax.all_to_all(copies, 'z', split_axis=0, concat_axis=0, tiled=True, axis...  6.52 us
    all_gather x1, blocking collectives, work(): gathered = lax.all_gather(column, 'xl', axis=0, tiled=True)  5.63 us
    ppermute x1, starting transfers between devices, local(): lax.ppermute(zeros[2], TM, [(t, t - 1) for t in range(2, groups, 2)])  2.3 us
    all_gather x1, blocking collectives, local(): lax.all_gather(jnp.where(core == 0, to_next, to_last), 'core', axis=0)  1.85 us
    transpose x1, local copies, waits for them, and re-layouts, local(): jnp.transpose(conv_weight, (1, 2, 3, 0, 4))  1.81 us
    pallas_call x1, Pallas kernels, local(): pl.pallas_call(attend_kernel, out_shape=jax.ShapeDtypeStruct((CELLS, 4 *...  1.38 us
  transfers between devices with their start and end apart: 3, of which 1 were waited for; matrix products, arithmetic and copies ran while one was open for 5% of the time, Pallas kernels for 1%

profile of v8, /device:TPU:24, one launch (start us, length us, event | category | flops | bytes accessed | tf_op | source)
XLA Modules:
  0.0 57.5 jit_solution(4933260420588596134)
XLA Ops:
  0.0 1.4 %broadcast_in_dim.11 = bf16[16,16,256]{2,1,0:T(8,128)(2,1)} broadcast(bf16[16,256]{1,0:T(8,128)(2,1)} %bitcast.18), dimensions={1,2} | broadcast | bytes 139264 | tf_op jit(solution)/shard_map/broadcast_in_dim | solution.py:121
  1.4 16.2 %all-to-all-start = ((bf16[16,16,256]{2,1,0:T(8,128)(2,1)}), bf16[16,16,256]{2,1,0:T(8,128)(2,1)S(1)}, u32[]{:S(2)}, u32[]{:S(2)}) async-start(bf16[16,16,256]{2,1,0:T(8,128)(2,1)} %broadcast_in_dim.11), calls=%async_computation | async-start | bytes 262144 | tf_op jit(solution)/shard_map/all_to_all | solution.py:122
  17.5 1.8 %copy.9 = bf16[4,4,4,16,512]{4,3,2,1,0:T(8,128)(2,1)S(1)} copy(bf16[4,4,4,16,512]{4,2,1,0,3:T(4,128)(2,1)} %bitcast.16) | data formatting | bytes 2097152 | tf_op jit(solution)/shard_map/transpose | solution.py:125
  19.3 0.8 %dynamic-slice_bitcast_fusion = (bf16[128,128]{1,0:T(8,128)(2,1)S(1)}, bf16[128,128]{1,0:T(8,128)(2,1)S(1)}) fusion(bf16[16,128,128]{2,1,0:T(8,128)(2,1)} %param.13, s32[]{:T(128)S(6)} %select_n.42, bf16[16,128,128]{2,1,0:T(8,128)(2,1)} %param.12), kind=kLoop, calls=%fused_computation.6 | loop fusion | bytes 131076 | tf_op jit(solution)/shard_map/jit(dynamic_index_in_dim)/squeeze | solution.py:128
  20.1 0.0 copy-start
  20.1 6.5 %all-to-all-done = bf16[16,16,256]{2,1,0:T(8,128)(2,1)S(1)} async-done(((bf16[16,16,256]{2,1,0:T(8,128)(2,1)}), bf16[16,16,256]{2,1,0:T(8,128)(2,1)S(1)}, u32[]{:S(2)}, u32[]{:S(2)}) %all-to-all-start) | async-done | bytes 131104 | tf_op jit(solution)/shard_map/all_to_all | solution.py:122
  26.6 0.0 copy-done
  26.6 1.3 %collective-permute-start = (bf16[16,8,128]{2,1,0:T(8,128)(2,1)S(1)}, bf16[16,8,128]{2,1,0:T(8,128)(2,1)S(1)}, u32[]{:S(2)}, u32[]{:S(2)}) collective-permute-start(bf16[16,8,128]{2,1,0:T(8,128)(2,1)S(1)} %get-tuple-element.37), channel_id=1, source_target_pairs={{32,64},{96,128},{160,192},{224,256},{288,320},{352,384},{416,448}... | collective-permute-start | bytes 98312 | tf_op jit(solution)/shard_map/ppermute | solution.py:160
  27.9 6.4 %conditional.3 = ((f32[2,16,8,128]{3,2,1,0:T(8,128)S(1)}, bf16[16,8,128]{2,1,0:T(8,128)(2,1)S(1)}, bf16[16,8,128]{2,1,0:T(8,128)(2,1)S(1)})) conditional(s32[]{:T(128)} %convert_element_type.11, () %tuple.19, (bf16[16,16,256]{2,1,0:T(8,128)(2,1)S(1)}, bf16[1024,512]{1,0:T(8,128)(2,1)S(1)}, f32[16,1]{0,1:T(1,128)S(1)}) %tuple.42), branch_computations={%region_2.3_spmd, %region_3.4_spmd} | conditional | bytes 393352 | solution.py:162
  27.9 0.1 copy.11.bias_ref
  28.0 5.6 %all_gather.9.latent_ref = bf16[32,16,256]{2,1,0:T(8,128)(2,1)S(1)} all-gather(bf16[16,16,256]{2,1,0:T(8,128)(2,1)S(1)} %get-tuple-element.21), channel_id=1, replica_groups=mesh['pair'=8,'core'=2,'xl'=2,'z'=16] {'xl'}, dimensions={0}, use_global_device_ids=true | all-gather | bytes 393216 | tf_op jit(solution)/shard_map/cond/branch_1_fun/all_gather | solution.py:138
  33.7 0.6 %conv.3 = (f32[2,16,8,128]{3,2,1,0:T(8,128)S(1)}, bf16[16,8,128]{2,1,0:T(8,128)(2,1)S(1)}, bf16[16,8,128]{2,1,0:T(8,128)(2,1)S(1)}) custom-call(bf16[1024,512]{1,0:T(8,128)(2,1)S(1)} %get-tuple-element.20.weight_ref, bf16[32,16,256]{2,1,0:T(8,128)(2,1)S(1)} %all_gather.9.latent_ref, f32[16,1]{1,0:T(8,128)S(1)} %copy.11.bias_ref), custom_call_target="tpu_custom_call" | custom-call | tf_op jit(solution)/shard_map/cond/branch_1_fun/conv/pallas_call | solution.py:140
  34.3 2.3 %collective-permute-start.1 = (bf16[16,8,128]{2,1,0:T(8,128)(2,1)S(1)}, bf16[16,8,128]{2,1,0:T(8,128)(2,1)S(1)}, u32[]{:S(2)}, u32[]{:S(2)}) collective-permute-start(bf16[16,8,128]{2,1,0:T(8,128)(2,1)S(1)} %get-tuple-element.43), channel_id=1, source_target_pairs={{64,32},{128,96},{192,160},{256,224},{320,288},{384,352},{448,416}... | collective-permute-start | bytes 98312 | tf_op jit(solution)/shard_map/ppermute | solution.py:165
  36.6 1.9 %all-gather = bf16[32,8,128]{2,1,0:T(8,128)(2,1)S(1)} all-gather(bf16[16,8,128]{2,1,0:T(8,128)(2,1)S(1)} %select_select_fusion), channel_id=2, replica_groups=mesh['pair'=8,'core'=2,'xl'=2,'z'=16] {'core'}, dimensions={0}, use_global_device_ids=true | all-gather | bytes 98304 | tf_op jit(solution)/shard_map/all_gather | solution.py:166
  38.5 0.0 collective-permute-done.1
  38.5 0.0 collective-permute-done
  38.5 17.6 %all_to_all.10.piece_ref = bf16[32,8,128]{2,1,0:T(8,128)(2,1)S(1)} all-to-all(bf16[32,8,128]{2,1,0:T(8,128)(2,1)S(1)} %bitcast.17), channel_id=1, replica_groups={{8,9,10,11,12,13,14,15,0,1,2,3,4,5,6,7,24,25,26,27,28,29,30,31,16,17,18..., dimensions={0} | all-to-all | bytes 131072 | tf_op jit(solution)/shard_map/all_to_all | solution.py:170
  56.1 1.4 %attend.1 = bf16[256,128]{1,0:T(8,128)(2,1)} custom-call(bf16[32,8,128]{2,1,0:T(8,128)(2,1)S(1)} %all_to_all.10.piece_ref, bf16[128,128]{1,0:T(8,128)(2,1)S(1)} %get-tuple-element.45.query_ref, bf16[128,128]{1,0:T(8,128)(2,1)S(1)} %get-tuple-element.46.key_ref), custom_call_target="tpu_custom_call" | custom-call | tf_op jit(solution)/shard_map/attend/pallas_call | solution.py:174
  (5 shorter events, 0.1 us)
Async XLA Ops:
  1.4 25.3 %all-to-all-start = ((bf16[16,16,256]{2,1,0:T(8,128)(2,1)}), bf16[16,16,256]{2,1,0:T(8,128)(2,1)S(1)}, u32[]{:S(2)}, u32[]{:S(2)}) async-start(bf16[16,16,256]{2,1,0:T(8,128)(2,1)} %broadcast_in_dim.11), calls=%async_computation | async-start | bytes 262144 | tf_op jit(solution)/shard_map/all_to_all | solution.py:122
  20.1 6.5 %copy-start = (f32[16]{0:T(128)S(1)}, f32[16]{0:T(128)}, u32[]{:S(2)}) copy-start(f32[16]{0:T(128)} %param.11) | copy-start | bytes 196
  26.6 11.9 %collective-permute-start = (bf16[16,8,128]{2,1,0:T(8,128)(2,1)S(1)}, bf16[16,8,128]{2,1,0:T(8,128)(2,1)S(1)}, u32[]{:S(2)}, u32[]{:S(2)}) collective-permute-start(bf16[16,8,128]{2,1,0:T(8,128)(2,1)S(1)} %get-tuple-element.37), channel_id=1, source_target_pairs={{32,64},{96,128},{160,192},{224,256},{288,320},{352,384},{416,448}... | collective-permute-start | bytes 98312 | tf_op jit(solution)/shard_map/ppermute | solution.py:160
  34.3 4.2 %collective-permute-start.1 = (bf16[16,8,128]{2,1,0:T(8,128)(2,1)S(1)}, bf16[16,8,128]{2,1,0:T(8,128)(2,1)S(1)}, u32[]{:S(2)}, u32[]{:S(2)}) collective-permute-start(bf16[16,8,128]{2,1,0:T(8,128)(2,1)S(1)} %get-tuple-element.43), channel_id=1, source_target_pairs={{64,32},{128,96},{192,160},{256,224},{320,288},{384,352},{448,416}... | collective-permute-start | bytes 98312 | tf_op jit(solution)/shard_map/ppermute | solution.py:165

commit v9 on v8

--- a/solution.py
+++ b/solution.py
@@ -13,7 +13,7 @@
 VMEM_LIMIT = 32 * 1024 * 1024
 
 
-FIRST_GATHER, FIRST_FRAMES = 11, 8
+FIRST_GATHER, FIRST_FRAMES = 10, 10
 
 
 def turned(order, first):

time: 58.5 us -> 58.4 us (level)
  starting transfers between devices: 19.7 us -> 20.6 us
  waiting for transfers between devices: 6.52 us -> 5.63 us
    all_to_all x1, starting transfers between devices: 16.2 us -> 17.1 us  [local(): lax.all_to_all(copies, 'z', split_axis=0, concat_axis=0, tiled=True, axis...]
    all_to_all x1, waiting for transfers between devices: 6.52 us -> 5.63 us  [local(): lax.all_to_all(copies, 'z', split_axis=0, concat_axis=0, tiled=True, axis...]
where the time goes in v9:
time: 58.4 us; the launch traced here: 57.6 us
  blocking collectives  25.2 us (43%)
  starting transfers between devices  20.6 us (35%)
  waiting for transfers between devices  5.63 us (10%)
  local copies, waits for them, and re-layouts  4.03 us (7%)
  Pallas kernels  2.04 us (3%)
    all_to_all x1, blocking collectives, local(): lax.all_to_all(frames.reshape(2 * channels, 8, 128), TILE, split_axis=0,...  17.7 us
    all_to_all x1, starting transfers between devices, local(): lax.all_to_all(copies, 'z', split_axis=0, concat_axis=0, tiled=True, axis...  17.1 us
    all_gather x1, blocking collectives, work(): gathered = lax.all_gather(column, 'xl', axis=0, tiled=True)  5.63 us
    all_to_all x1, waiting for transfers between devices, local(): lax.all_to_all(copies, 'z', split_axis=0, concat_axis=0, tiled=True, axis...  5.63 us
    ppermute x1, starting transfers between devices, local(): lax.ppermute(zeros[2], TM, [(t, t - 1) for t in range(2, groups, 2)])  2.27 us
    all_gather x1, blocking collectives, local(): lax.all_gather(jnp.where(core == 0, to_next, to_last), 'core', axis=0)  1.85 us
    transpose x1, local copies, waits for them, and re-layouts, local(): jnp.transpose(conv_weight, (1, 2, 3, 0, 4))  1.81 us
    pallas_call x1, Pallas kernels, local(): pl.pallas_call(attend_kernel, out_shape=jax.ShapeDtypeStruct((CELLS, 4 *...  1.41 us
  transfers between devices with their start and end apart: 3, of which 1 were waited for; matrix products, arithmetic and copies ran while one was open for 5% of the time, Pallas kernels for 1%

profile of v9, /device:TPU:24, one launch (start us, length us, event | category | flops | bytes accessed | tf_op | source)
XLA Modules:
  0.0 57.6 jit_solution(12770093884181175474)
XLA Ops:
  0.0 1.4 %broadcast_in_dim.11 = bf16[16,16,256]{2,1,0:T(8,128)(2,1)} broadcast(bf16[16,256]{1,0:T(8,128)(2,1)} %bitcast.18), dimensions={1,2} | broadcast | bytes 139264 | tf_op jit(solution)/shard_map/broadcast_in_dim | solution.py:121
  1.4 17.1 %all-to-all-start = ((bf16[16,16,256]{2,1,0:T(8,128)(2,1)}), bf16[16,16,256]{2,1,0:T(8,128)(2,1)S(1)}, u32[]{:S(2)}, u32[]{:S(2)}) async-start(bf16[16,16,256]{2,1,0:T(8,128)(2,1)} %broadcast_in_dim.11), calls=%async_computation | async-start | bytes 262144 | tf_op jit(solution)/shard_map/all_to_all | solution.py:122
  18.4 1.8 %copy.9 = bf16[4,4,4,16,512]{4,3,2,1,0:T(8,128)(2,1)S(1)} copy(bf16[4,4,4,16,512]{4,2,1,0,3:T(4,128)(2,1)} %bitcast.16) | data formatting | bytes 2097152 | tf_op jit(solution)/shard_map/transpose | solution.py:125
  20.2 0.8 %dynamic-slice_bitcast_fusion = (bf16[128,128]{1,0:T(8,128)(2,1)S(1)}, bf16[128,128]{1,0:T(8,128)(2,1)S(1)}) fusion(bf16[16,128,128]{2,1,0:T(8,128)(2,1)} %param.13, s32[]{:T(128)S(6)} %select_n.42, bf16[16,128,128]{2,1,0:T(8,128)(2,1)} %param.12), kind=kLoop, calls=%fused_computation.6 | loop fusion | bytes 131076 | tf_op jit(solution)/shard_map/jit(dynamic_index_in_dim)/squeeze | solution.py:128
  21.0 0.0 copy-start
  21.0 5.6 %all-to-all-done = bf16[16,16,256]{2,1,0:T(8,128)(2,1)S(1)} async-done(((bf16[16,16,256]{2,1,0:T(8,128)(2,1)}), bf16[16,16,256]{2,1,0:T(8,128)(2,1)S(1)}, u32[]{:S(2)}, u32[]{:S(2)}) %all-to-all-start) | async-done | bytes 131104 | tf_op jit(solution)/shard_map/all_to_all | solution.py:122
  26.6 0.0 copy-done
  26.6 1.3 %collective-permute-start = (bf16[16,8,128]{2,1,0:T(8,128)(2,1)S(1)}, bf16[16,8,128]{2,1,0:T(8,128)(2,1)S(1)}, u32[]{:S(2)}, u32[]{:S(2)}) collective-permute-start(bf16[16,8,128]{2,1,0:T(8,128)(2,1)S(1)} %get-tuple-element.37), channel_id=1, source_target_pairs={{32,64},{96,128},{160,192},{224,256},{288,320},{352,384},{416,448}... | collective-permute-start | bytes 98312 | tf_op jit(solution)/shard_map/ppermute | solution.py:160
  27.9 6.4 %conditional.3 = ((f32[2,16,8,128]{3,2,1,0:T(8,128)S(1)}, bf16[16,8,128]{2,1,0:T(8,128)(2,1)S(1)}, bf16[16,8,128]{2,1,0:T(8,128)(2,1)S(1)})) conditional(s32[]{:T(128)} %convert_element_type.11, () %tuple.19, (bf16[16,16,256]{2,1,0:T(8,128)(2,1)S(1)}, bf16[1024,512]{1,0:T(8,128)(2,1)S(1)}, f32[16,1]{0,1:T(1,128)S(1)}) %tuple.42), branch_computations={%region_2.3_spmd, %region_3.4_spmd} | conditional | bytes 393352 | solution.py:162
  28.0 0.1 copy.11.bias_ref
  28.0 5.6 %all_gather.9.latent_ref = bf16[32,16,256]{2,1,0:T(8,128)(2,1)S(1)} all-gather(bf16[16,16,256]{2,1,0:T(8,128)(2,1)S(1)} %get-tuple-element.21), channel_id=1, replica_groups=mesh['pair'=8,'core'=2,'xl'=2,'z'=16] {'xl'}, dimensions={0}, use_global_device_ids=true | all-gather | bytes 393216 | tf_op jit(solution)/shard_map/cond/branch_1_fun/all_gather | solution.py:138
  33.7 0.6 %conv.3 = (f32[2,16,8,128]{3,2,1,0:T(8,128)S(1)}, bf16[16,8,128]{2,1,0:T(8,128)(2,1)S(1)}, bf16[16,8,128]{2,1,0:T(8,128)(2,1)S(1)}) custom-call(bf16[1024,512]{1,0:T(8,128)(2,1)S(1)} %get-tuple-element.20.weight_ref, bf16[32,16,256]{2,1,0:T(8,128)(2,1)S(1)} %all_gather.9.latent_ref, f32[16,1]{1,0:T(8,128)S(1)} %copy.11.bias_ref), custom_call_target="tpu_custom_call" | custom-call | tf_op jit(solution)/shard_map/cond/branch_1_fun/conv/pallas_call | solution.py:140
  34.3 2.3 %collective-permute-start.1 = (bf16[16,8,128]{2,1,0:T(8,128)(2,1)S(1)}, bf16[16,8,128]{2,1,0:T(8,128)(2,1)S(1)}, u32[]{:S(2)}, u32[]{:S(2)}) collective-permute-start(bf16[16,8,128]{2,1,0:T(8,128)(2,1)S(1)} %get-tuple-element.43), channel_id=1, source_target_pairs={{64,32},{128,96},{192,160},{256,224},{320,288},{384,352},{448,416}... | collective-permute-start | bytes 98312 | tf_op jit(solution)/shard_map/ppermute | solution.py:165
  36.6 1.9 %all-gather = bf16[32,8,128]{2,1,0:T(8,128)(2,1)S(1)} all-gather(bf16[16,8,128]{2,1,0:T(8,128)(2,1)S(1)} %select_select_fusion), channel_id=2, replica_groups=mesh['pair'=8,'core'=2,'xl'=2,'z'=16] {'core'}, dimensions={0}, use_global_device_ids=true | all-gather | bytes 98304 | tf_op jit(solution)/shard_map/all_gather | solution.py:166
  38.5 0.0 collective-permute-done.1
  38.5 0.0 collective-permute-done
  38.5 17.7 %all_to_all.10.piece_ref = bf16[32,8,128]{2,1,0:T(8,128)(2,1)S(1)} all-to-all(bf16[32,8,128]{2,1,0:T(8,128)(2,1)S(1)} %bitcast.17), channel_id=1, replica_groups={{10,11,12,13,14,15,0,1,2,3,4,5,6,7,8,9,26,27,28,29,30,31,16,17,18,19,20..., dimensions={0} | all-to-all | bytes 131072 | tf_op jit(solution)/shard_map/all_to_all | solution.py:170
  56.2 1.4 %attend.1 = bf16[256,128]{1,0:T(8,128)(2,1)} custom-call(bf16[32,8,128]{2,1,0:T(8,128)(2,1)S(1)} %all_to_all.10.piece_ref, bf16[128,128]{1,0:T(8,128)(2,1)S(1)} %get-tuple-element.45.query_ref, bf16[128,128]{1,0:T(8,128)(2,1)S(1)} %get-tuple-element.46.key_ref), custom_call_target="tpu_custom_call" | custom-call | tf_op jit(solution)/shard_map/attend/pallas_call | solution.py:174
  (5 shorter events, 0.1 us)
Async XLA Ops:
  1.4 25.3 %all-to-all-start = ((bf16[16,16,256]{2,1,0:T(8,128)(2,1)}), bf16[16,16,256]{2,1,0:T(8,128)(2,1)S(1)}, u32[]{:S(2)}, u32[]{:S(2)}) async-start(bf16[16,16,256]{2,1,0:T(8,128)(2,1)} %broadcast_in_dim.11), calls=%async_computation | async-start | bytes 262144 | tf_op jit(solution)/shard_map/all_to_all | solution.py:122
  21.0 5.6 %copy-start = (f32[16]{0:T(128)S(1)}, f32[16]{0:T(128)}, u32[]{:S(2)}) copy-start(f32[16]{0:T(128)} %param.11) | copy-start | bytes 196
  26.6 11.8 %collective-permute-start = (bf16[16,8,128]{2,1,0:T(8,128)(2,1)S(1)}, bf16[16,8,128]{2,1,0:T(8,128)(2,1)S(1)}, u32[]{:S(2)}, u32[]{:S(2)}) collective-permute-start(bf16[16,8,128]{2,1,0:T(8,128)(2,1)S(1)} %get-tuple-element.37), channel_id=1, source_target_pairs={{32,64},{96,128},{160,192},{224,256},{288,320},{352,384},{416,448}... | collective-permute-start | bytes 98312 | tf_op jit(solution)/shard_map/ppermute | solution.py:160
  34.3 4.2 %collective-permute-start.1 = (bf16[16,8,128]{2,1,0:T(8,128)(2,1)S(1)}, bf16[16,8,128]{2,1,0:T(8,128)(2,1)S(1)}, u32[]{:S(2)}, u32[]{:S(2)}) collective-permute-start(bf16[16,8,128]{2,1,0:T(8,128)(2,1)S(1)} %get-tuple-element.43), channel_id=1, source_target_pairs={{64,32},{128,96},{192,160},{256,224},{320,288},{384,352},{448,416}... | collective-permute-start | bytes 98312 | tf_op jit(solution)/shard_map/ppermute | solution.py:165

commit v10 on v9

--- a/solution.py
+++ b/solution.py
@@ -98,8 +98,8 @@
             start = parity * channels + target
             turned_ref[start : start + size, columns] = wide_ref[source : source + size, place, :]
     across = turned_ref[...]
-    wide = across.T
-    tokens, across = wide.astype(jnp.bfloat16), across.astype(jnp.bfloat16)
+    wide, across = across, across.astype(jnp.bfloat16)
+    tokens = across.T
     contract_first = (((0,), (0,)), ((), ()))
     queries = lax.dot_general(query_ref[...], across, contract_first, preferred_element_type=jnp.float32)
     keys = jnp.dot(tokens, key_ref[...], preferred_element_type=jnp.float32)
@@ -108,7 +108,7 @@
     raised = jnp.exp(scores - jnp.max(scores, axis=0, keepdims=True))
     weights = (raised / jnp.sum(raised, axis=0, keepdims=True)).astype(jnp.bfloat16)
     mixed = jnp.dot(across, weights, preferred_element_type=jnp.float32)
-    out_ref[...] = (wide + mixed.T).astype(jnp.bfloat16)
+    out_ref[...] = (wide + mixed).T.astype(jnp.bfloat16)
 
 
 def local(latent, conv_weight, conv_bias, query_weight, key_weight):

time: 58.4 us -> 58.4 us (level)
  no operation moved by 1% of the time
where the time goes in v10:
time: 58.4 us; the launch traced here: 57.6 us
  blocking collectives  25.2 us (43%)
  starting transfers between devices  20.6 us (35%)
  waiting for transfers between devices  5.63 us (10%)
  local copies, waits for them, and re-layouts  4.03 us (7%)
  Pallas kernels  2.04 us (3%)
    all_to_all x1, blocking collectives, local(): lax.all_to_all(frames.reshape(2 * channels, 8, 128), TILE, split_axis=0,...  17.7 us
    all_to_all x1, starting transfers between devices, local(): lax.all_to_all(copies, 'z', split_axis=0, concat_axis=0, tiled=True, axis...  17.1 us
    all_gather x1, blocking collectives, work(): gathered = lax.all_gather(column, 'xl', axis=0, tiled=True)  5.63 us
    all_to_all x1, waiting for transfers between devices, local(): lax.all_to_all(copies, 'z', split_axis=0, concat_axis=0, tiled=True, axis...  5.63 us
    ppermute x1, starting transfers between devices, local(): lax.ppermute(zeros[2], TM, [(t, t - 1) for t in range(2, groups, 2)])  2.27 us
    all_gather x1, blocking collectives, local(): lax.all_gather(jnp.where(core == 0, to_next, to_last), 'core', axis=0)  1.85 us
    transpose x1, local copies, waits for them, and re-layouts, local(): jnp.transpose(conv_weight, (1, 2, 3, 0, 4))  1.81 us
    pallas_call x1, Pallas kernels, local(): pl.pallas_call(attend_kernel, out_shape=jax.ShapeDtypeStruct((CELLS, 4 *...  1.41 us
  transfers between devices with their start and end apart: 3, of which 1 were waited for; matrix products, arithmetic and copies ran while one was open for 5% of the time, Pallas kernels for 1%

profile of v10, /device:TPU:24, one launch (start us, length us, event | category | flops | bytes accessed | tf_op | source)
XLA Modules:
  0.0 57.6 jit_solution(2943819246238130661)
XLA Ops:
  0.0 1.4 %broadcast_in_dim.11 = bf16[16,16,256]{2,1,0:T(8,128)(2,1)} broadcast(bf16[16,256]{1,0:T(8,128)(2,1)} %bitcast.18), dimensions={1,2} | broadcast | bytes 139264 | tf_op jit(solution)/shard_map/broadcast_in_dim | solution.py:121
  1.4 17.1 %all-to-all-start = ((bf16[16,16,256]{2,1,0:T(8,128)(2,1)}), bf16[16,16,256]{2,1,0:T(8,128)(2,1)S(1)}, u32[]{:S(2)}, u32[]{:S(2)}) async-start(bf16[16,16,256]{2,1,0:T(8,128)(2,1)} %broadcast_in_dim.11), calls=%async_computation | async-start | bytes 262144 | tf_op jit(solution)/shard_map/all_to_all | solution.py:122
  18.4 1.8 %copy.9 = bf16[4,4,4,16,512]{4,3,2,1,0:T(8,128)(2,1)S(1)} copy(bf16[4,4,4,16,512]{4,2,1,0,3:T(4,128)(2,1)} %bitcast.16) | data formatting | bytes 2097152 | tf_op jit(solution)/shard_map/transpose | solution.py:125
  20.2 0.8 %dynamic-slice_bitcast_fusion = (bf16[128,128]{1,0:T(8,128)(2,1)S(1)}, bf16[128,128]{1,0:T(8,128)(2,1)S(1)}) fusion(bf16[16,128,128]{2,1,0:T(8,128)(2,1)} %param.13, s32[]{:T(128)S(6)} %select_n.42, bf16[16,128,128]{2,1,0:T(8,128)(2,1)} %param.12), kind=kLoop, calls=%fused_computation.6 | loop fusion | bytes 131076 | tf_op jit(solution)/shard_map/jit(dynamic_index_in_dim)/squeeze | solution.py:128
  21.0 0.0 copy-start
  21.0 5.6 %all-to-all-done = bf16[16,16,256]{2,1,0:T(8,128)(2,1)S(1)} async-done(((bf16[16,16,256]{2,1,0:T(8,128)(2,1)}), bf16[16,16,256]{2,1,0:T(8,128)(2,1)S(1)}, u32[]{:S(2)}, u32[]{:S(2)}) %all-to-all-start) | async-done | bytes 131104 | tf_op jit(solution)/shard_map/all_to_all | solution.py:122
  26.6 0.0 copy-done
  26.6 1.3 %collective-permute-start = (bf16[16,8,128]{2,1,0:T(8,128)(2,1)S(1)}, bf16[16,8,128]{2,1,0:T(8,128)(2,1)S(1)}, u32[]{:S(2)}, u32[]{:S(2)}) collective-permute-start(bf16[16,8,128]{2,1,0:T(8,128)(2,1)S(1)} %get-tuple-element.37), channel_id=1, source_target_pairs={{32,64},{96,128},{160,192},{224,256},{288,320},{352,384},{416,448}... | collective-permute-start | bytes 98312 | tf_op jit(solution)/shard_map/ppermute | solution.py:160
  27.9 6.4 %conditional.3 = ((f32[2,16,8,128]{3,2,1,0:T(8,128)S(1)}, bf16[16,8,128]{2,1,0:T(8,128)(2,1)S(1)}, bf16[16,8,128]{2,1,0:T(8,128)(2,1)S(1)})) conditional(s32[]{:T(128)} %convert_element_type.11, () %tuple.19, (bf16[16,16,256]{2,1,0:T(8,128)(2,1)S(1)}, bf16[1024,512]{1,0:T(8,128)(2,1)S(1)}, f32[16,1]{0,1:T(1,128)S(1)}) %tuple.42), branch_computations={%region_2.3_spmd, %region_3.4_spmd} | conditional | bytes 393352 | solution.py:162
  28.0 0.1 copy.11.bias_ref
  28.0 5.6 %all_gather.9.latent_ref = bf16[32,16,256]{2,1,0:T(8,128)(2,1)S(1)} all-gather(bf16[16,16,256]{2,1,0:T(8,128)(2,1)S(1)} %get-tuple-element.21), channel_id=1, replica_groups=mesh['pair'=8,'core'=2,'xl'=2,'z'=16] {'xl'}, dimensions={0}, use_global_device_ids=true | all-gather | bytes 393216 | tf_op jit(solution)/shard_map/cond/branch_1_fun/all_gather | solution.py:138
  33.7 0.6 %conv.3 = (f32[2,16,8,128]{3,2,1,0:T(8,128)S(1)}, bf16[16,8,128]{2,1,0:T(8,128)(2,1)S(1)}, bf16[16,8,128]{2,1,0:T(8,128)(2,1)S(1)}) custom-call(bf16[1024,512]{1,0:T(8,128)(2,1)S(1)} %get-tuple-element.20.weight_ref, bf16[32,16,256]{2,1,0:T(8,128)(2,1)S(1)} %all_gather.9.latent_ref, f32[16,1]{1,0:T(8,128)S(1)} %copy.11.bias_ref), custom_call_target="tpu_custom_call" | custom-call | tf_op jit(solution)/shard_map/cond/branch_1_fun/conv/pallas_call | solution.py:140
  34.3 2.3 %collective-permute-start.1 = (bf16[16,8,128]{2,1,0:T(8,128)(2,1)S(1)}, bf16[16,8,128]{2,1,0:T(8,128)(2,1)S(1)}, u32[]{:S(2)}, u32[]{:S(2)}) collective-permute-start(bf16[16,8,128]{2,1,0:T(8,128)(2,1)S(1)} %get-tuple-element.43), channel_id=1, source_target_pairs={{64,32},{128,96},{192,160},{256,224},{320,288},{384,352},{448,416}... | collective-permute-start | bytes 98312 | tf_op jit(solution)/shard_map/ppermute | solution.py:165
  36.6 1.9 %all-gather = bf16[32,8,128]{2,1,0:T(8,128)(2,1)S(1)} all-gather(bf16[16,8,128]{2,1,0:T(8,128)(2,1)S(1)} %select_select_fusion), channel_id=2, replica_groups=mesh['pair'=8,'core'=2,'xl'=2,'z'=16] {'core'}, dimensions={0}, use_global_device_ids=true | all-gather | bytes 98304 | tf_op jit(solution)/shard_map/all_gather | solution.py:166
  38.5 0.0 collective-permute-done.1
  38.5 0.0 collective-permute-done
  38.5 17.7 %all_to_all.10.piece_ref = bf16[32,8,128]{2,1,0:T(8,128)(2,1)S(1)} all-to-all(bf16[32,8,128]{2,1,0:T(8,128)(2,1)S(1)} %bitcast.17), channel_id=1, replica_groups={{10,11,12,13,14,15,0,1,2,3,4,5,6,7,8,9,26,27,28,29,30,31,16,17,18,19,20..., dimensions={0} | all-to-all | bytes 131072 | tf_op jit(solution)/shard_map/all_to_all | solution.py:170
  56.2 1.4 %attend.1 = bf16[256,128]{1,0:T(8,128)(2,1)} custom-call(bf16[32,8,128]{2,1,0:T(8,128)(2,1)S(1)} %all_to_all.10.piece_ref, bf16[128,128]{1,0:T(8,128)(2,1)S(1)} %get-tuple-element.45.query_ref, bf16[128,128]{1,0:T(8,128)(2,1)S(1)} %get-tuple-element.46.key_ref), custom_call_target="tpu_custom_call" | custom-call | tf_op jit(solution)/shard_map/attend/pallas_call | solution.py:174
  (5 shorter events, 0.1 us)
Async XLA Ops:
  1.4 25.3 %all-to-all-start = ((bf16[16,16,256]{2,1,0:T(8,128)(2,1)}), bf16[16,16,256]{2,1,0:T(8,128)(2,1)S(1)}, u32[]{:S(2)}, u32[]{:S(2)}) async-start(bf16[16,16,256]{2,1,0:T(8,128)(2,1)} %broadcast_in_dim.11), calls=%async_computation | async-start | bytes 262144 | tf_op jit(solution)/shard_map/all_to_all | solution.py:122
  21.0 5.6 %copy-start = (f32[16]{0:T(128)S(1)}, f32[16]{0:T(128)}, u32[]{:S(2)}) copy-start(f32[16]{0:T(128)} %param.11) | copy-start | bytes 196
  26.6 11.8 %collective-permute-start = (bf16[16,8,128]{2,1,0:T(8,128)(2,1)S(1)}, bf16[16,8,128]{2,1,0:T(8,128)(2,1)S(1)}, u32[]{:S(2)}, u32[]{:S(2)}) collective-permute-start(bf16[16,8,128]{2,1,0:T(8,128)(2,1)S(1)} %get-tuple-element.37), channel_id=1, source_target_pairs={{32,64},{96,128},{160,192},{224,256},{288,320},{352,384},{416,448}... | collective-permute-start | bytes 98312 | tf_op jit(solution)/shard_map/ppermute | solution.py:160
  34.3 4.2 %collective-permute-start.1 = (bf16[16,8,128]{2,1,0:T(8,128)(2,1)S(1)}, bf16[16,8,128]{2,1,0:T(8,128)(2,1)S(1)}, u32[]{:S(2)}, u32[]{:S(2)}) collective-permute-start(bf16[16,8,128]{2,1,0:T(8,128)(2,1)S(1)} %get-tuple-element.43), channel_id=1, source_target_pairs={{64,32},{128,96},{192,160},{256,224},{320,288},{384,352},{448,416}... | collective-permute-start | bytes 98312 | tf_op jit(solution)/shard_map/ppermute | solution.py:165
